TPU v7x, 128 devices: a whole 4x4x4 slice. The times are simulated.
128 devices in a mesh: span: 8 (over y_hi, z), seq: 16 (over x, y_lo, core).
Axes of the slice: x: 4, y: 4 (y_hi: 2, y_lo: 2; y = y_hi * 2 + y_lo), z: 4, core: 2. Of those that a mesh axis runs over, the one named last changes fastest.
Arguments:
- queries: bfloat16 [8, 512, 4096], P('span', 'seq')
- keys: bfloat16 [8, 512, 4096], P('span', 'seq')
- values: bfloat16 [8, 512, 4096], P('span', 'seq'), may hold values from -6 to 6
- gate_table: float32 [50, 4096], replicated, may hold values from -6 to 6
- levels: int32 [8], replicated, may hold values from 0 to 49
- span_rank: int32 [8], replicated, may hold values from 0 to 7, each once
Outputs:
- gated: bfloat16 [8, 512, 4096], P('span', 'seq')
Inputs may be any that keep to these rules, and one draw needn't show every extreme that they name: `span_rank`: each span has one place in time, each place used once.
All inputs are finite; a program needn't handle non-finite values.
Results may differ from a plain program's by a relative error of at most 0.012.
Values may be sent and summed in bfloat16 or wider, within the bound.
No kernel may reach another device: no remote copies, remote signals or barrier semaphores. Data moves between devices by JAX's collectives and lax.ppermute only.
A program may use at most 192 MiB of HBM per device.

v0:
```python
import jax
import jax.numpy as jnp
from jax import lax
from jax.sharding import PartitionSpec as P

HD = 128


def pick_entry(table, index):
    places = jnp.arange(table.shape[0], dtype=jnp.int32)
    return jnp.sum(jnp.where(places == index, table, 0))


def fold_step(query_three, span_len, span_rank, my_rank, head_dim):
    score_scale = 1.0 / head_dim**0.5
    heads_here = query_three.shape[1]
    places = jnp.arange(span_rank.shape[0], dtype=jnp.int32)

    def step(carry, pieces, start):
        key_piece, value_piece = pieces
        count = key_piece.shape[0]
        key_span = jnp.arange(count, dtype=jnp.int32) // span_len
        key_rank = jnp.sum(
            jnp.where(key_span[:, None] == places[None, :], span_rank[None, :], 0), axis=1
        )
        seen = key_rank <= my_rank
        run_top, run_total, run_acc = carry
        key_three = key_piece.reshape(count, heads_here, head_dim)
        value_three = value_piece.reshape(count, heads_here, head_dim)
        visible = seen[None, None, :]
        scores = (
            jnp.einsum("qhd,khd->hqk", query_three, key_three, preferred_element_type=jnp.float32)
            * score_scale
        )
        masked = jnp.where(visible, scores, -1e30)
        new_top = jnp.maximum(run_top, jnp.max(masked, axis=2))
        expo = jnp.where(visible, jnp.exp(masked - new_top[:, :, None]), 0.0)
        new_total = jnp.sum(expo, axis=2)
        new_acc = jnp.einsum(
            "hqk,khd->hqd",
            expo.astype(jnp.bfloat16),
            value_three,
            preferred_element_type=jnp.float32,
        )
        return (new_top, new_total, new_acc)

    return step


def attend_rows(query_rows, fold_call, head_dim):
    rows = query_rows.shape[0]
    heads_here = query_rows.shape[1] // head_dim
    query_three = query_rows.reshape(rows, heads_here, head_dim)
    start_carry = (
        jnp.full((heads_here, rows), -1e30, jnp.float32),
        jnp.zeros((heads_here, rows), jnp.float32),
        jnp.zeros((heads_here, rows, head_dim), jnp.float32),
    )
    run_top, run_total, run_acc = fold_call(query_three, start_carry)
    attended = run_acc / run_total[:, :, None]
    return attended.transpose(1, 0, 2).reshape(rows, heads_here * head_dim).astype(jnp.bfloat16)


def local(queries, keys, values, gate_table, levels, span_rank):
    head_dim = HD
    my_span = lax.axis_index("span")
    my_rank = pick_entry(span_rank, my_span)
    my_level = pick_entry(levels, my_span)
    query_local = queries[0]
    key_local = keys[0]
    value_local = values[0]
    span_len = query_local.shape[0] * lax.axis_size("seq")

    def fold_call(query_three, start_carry):
        step = fold_step(query_three, span_len, span_rank, my_rank, head_dim)
        return step(
            start_carry,
            (
                lax.all_gather(key_local, ("span", "seq"), axis=0, tiled=True),
                lax.all_gather(value_local, ("span", "seq"), axis=0, tiled=True),
            ),
            jnp.int32(0),
        )

    attended = attend_rows(query_local, fold_call, head_dim)
    gate_row = lax.dynamic_index_in_dim(gate_table, my_level, 0, keepdims=False)
    gated = (gate_row[None, :] * attended.astype(jnp.float32)).astype(jnp.bfloat16)
    return gated[None]


def solution(mesh):
    return jax.shard_map(
        local,
        mesh=mesh,
        in_specs=(
            P("span", "seq", None),
            P("span", "seq", None),
            P("span", "seq", None),
            P(),
            P(),
            P(),
        ),
        out_specs=P("span", "seq", None),
        check_vma=False,
    )
```

profile of v0, /device:TPU:0, one launch (start us, length us, event | category | flops | bytes accessed | tf_op | source)
XLA Modules:
  0.0 558.4 jit_solution(13296339022092998667)
XLA Ops:
  6.5 0.0 copy-start
  6.5 0.0 all-gather.5.cloned.1.call-start
  6.5 0.7 all-gather.5.cloned.1.call-update
  7.3 0.0 all-gather.7.cloned.1.call-start
  7.3 0.7 all-gather.7.cloned.1.call-update
  8.0 1.0 copy.28
  9.0 1.3 fusion.27
  12.3 1.3 fusion.28
  13.6 0.8 select_reduce_fusion
  14.3 0.7 broadcast_compare_fusion
  15.0 0.0 copy-done
  15.0 234.1 %all-gather.5.cloned.1.call-done = bf16[1,4096,4096]{2,1,0:T(8,128)(2,1)} async-done(((bf16[1,32,4096]{2,1,0:T(8,128)(2,1)}), bf16[1,4096,4096]{2,1,0:T(8,128)(2,1)}) %all-gather.5.cloned.1.call-update) | async-done | bytes 33554448 | tf_op jit(solution)/shard_map/all_gather | solution.py:79
  249.2 40.8 %copy.20 = bf16[1,4096,4096]{1,2,0:T(8,128)(2,1)} copy(bf16[1,4096,4096]{2,1,0:T(8,128)(2,1)} %all-gather.5.cloned.1.call-done) | data formatting | bytes 67108864 | tf_op jit(solution)/shard_map/all_gather | solution.py:79
  289.9 19.9 %fusion = (f32[32,32]{1,0:T(8,128)S(1)}, f32[32,32,4096]{2,1,0:T(8,128)}) fusion(pred[4096]{0:T(1024)(128)(4,1)S(1)} %broadcast_compare_fusion, bf16[4096,32,128]{0,2,1:T(8,128)(2,1)} %bitcast.17, bf16[32,32,128]{2,1,0:T(8,128)(2,1)S(1)} %bitcast.19), kind=kOutput, calls=%fused_computation.2 | convolution fusion | flops 1086323712 | bytes 50601984 | tf_op jit(solution)/shard_map/qhd,khd->hqk/dot_general | solution.py:32
  309.8 8.5 %fusion.1 = f32[32,32]{1,0:T(8,128)S(1)} fusion(f32[32,32,4096]{2,1,0:T(8,128)} %get-tuple-element.6, f32[32,32]{1,0:T(8,128)S(1)} %broadcast_maximum_fusion, pred[4096]{0:T(1024)(128)(4,1)S(1)} %broadcast_compare_fusion), kind=kLoop, calls=%fused_computation.3 | loop fusion | flops 20970496 | bytes 16789504 | tf_op jit(solution)/shard_map/reduce_sum | solution.py:38
  318.3 168.0 %all-gather.7.cloned.1.call-done = bf16[1,4096,4096]{2,1,0:T(8,128)(2,1)} async-done(((bf16[1,32,4096]{2,1,0:T(8,128)(2,1)}), bf16[1,4096,4096]{2,1,0:T(8,128)(2,1)}) %all-gather.7.cloned.1.call-update) | async-done | bytes 33554448 | tf_op jit(solution)/shard_map/all_gather | solution.py:80
  486.3 44.4 %copy.23 = bf16[1,4096,4096]{1,2,0:T(8,128)(2,1)} copy(bf16[1,4096,4096]{2,1,0:T(8,128)(2,1)} %all-gather.7.cloned.1.call-done) | data formatting | bytes 67108864 | tf_op jit(solution)/shard_map/all_gather | solution.py:80
  530.8 0.0 copy-start.1
  530.8 19.6 %fusion.19 = f32[32,32,128]{2,0,1:T(8,128)S(1)} fusion(bf16[4096,32,128]{0,2,1:T(8,128)(2,1)} %bitcast.18, f32[32,32,4096]{2,1,0:T(8,128)} %get-tuple-element.6, f32[32,32]{1,0:T(8,128)S(1)} %broadcast_maximum_fusion, pred[4096]{0:T(1024)(128)(4,1)S(1)} %broadcast_compare_fusion, f32[32,32]{0,1:T(8,128)S(1)} %bitcast.22), kind=kOutput, calls=%fused_computation.14 | convolution fusion | flops 1095106560 | bytes 50868224 | tf_op jit(solution)/shard_map/hqk,khd->hqd/dot_general | solution.py:39
  550.4 0.3 copy.25
  550.7 0.1 reshape.76
  550.8 0.7 multiply_convert_fusion
  551.5 0.0 copy-done.1
  (3 shorter events, 0.0 us)
Async XLA Ops:
  6.5 8.4 %copy-start = (f32[50,4096]{1,0:T(8,128)S(1)}, f32[50,4096]{1,0:T(8,128)}, u32[]{:S(2)}) copy-start(f32[50,4096]{1,0:T(8,128)} %param.9) | copy-start | bytes 2457604
  6.5 242.6 %all-gather.5.cloned.1.call-start = ((), (), s32[]{:S(2)}) async-start(), calls=%async_computation | async-start | bytes 33816576 | tf_op jit(solution)/shard_map/all_gather | solution.py:79
  7.3 479.1 %all-gather.7.cloned.1.call-start = ((), (), s32[]{:S(2)}) async-start(), calls=%async_computation.1 | async-start | bytes 33816576 | tf_op jit(solution)/shard_map/all_gather | solution.py:80
  530.8 20.8 %copy-start.1 = (f32[50,4096]{1,0:T(8,128)S(1)}, f32[50,4096]{1,0:T(8,128)}, u32[]{:S(2)}) copy-start(f32[50,4096]{1,0:T(8,128)} %param.9) | copy-start | bytes 2457604
Sparse Core Ops, SparseCore 0:
  9.1 240.0 all-gather.4
  250.9 235.4 all-gather.6
where the time goes:
time: 561 us; the launch traced here: 558 us
  waiting for transfers between devices  404 us (72%)
  local copies, waits for them, and re-layouts  86.6 us (15%)
  matrix products  39.5 us (7%)
  between operations  15.4 us (3%)
  other arithmetic  13.3 us (2%)
    all_gather x1, waiting for transfers between devices, fold_call(): lax.all_gather(key_local, ('span', 'seq'), axis=0, tiled=True)  234 us
    all_gather x1, waiting for transfers between devices, fold_call(): lax.all_gather(value_local, ('span', 'seq'), axis=0, tiled=True)  168 us
    all_gather x1, local copies, waits for them, and re-layouts, fold_call(): lax.all_gather(value_local, ('span', 'seq'), axis=0, tiled=True)  44.4 us
    all_gather x1, local copies, waits for them, and re-layouts, fold_call(): lax.all_gather(key_local, ('span', 'seq'), axis=0, tiled=True)  40.8 us
    dot_general x1, matrix products, step(): jnp.einsum('qhd,khd->hqk', query_three, key_three, preferred_element_type...  19.9 us
    dot_general x1, matrix products, step(): jnp.einsum('hqk,khd->hqd', expo.astype(jnp.bfloat16), value_three, prefer...  19.6 us
  transfers between devices with their start and end apart: 2, of which 2 were waited for; matrix products, arithmetic and copies ran while one was open for 13% of the time, Pallas kernels for 0%

commit v1 on v0

v1 whole, which is shorter than its diff:
```python
import functools

import jax
import jax.numpy as jnp
from jax import lax
from jax.experimental import pallas as pl
from jax.experimental.pallas import tpu as pltpu
from jax.sharding import Mesh
from jax.sharding import PartitionSpec as P

HD = 128
AXES = ("yh", "z", "x", "yl", "c")
SIZES = (2, 4, 4, 2, 2)
WIDE = ("yh", "z", "x")
NEAR = ("yl", "c")
MIB = 1 << 20


def pack_body(q_ref, k_ref, v_ref, o_ref):
    heads, rows3, hd = o_ref.shape
    rows = rows3 // 3
    for h in range(heads):
        cols = slice(h * hd, (h + 1) * hd)
        o_ref[h, 0:rows, :] = q_ref[:, cols]
        o_ref[h, rows : 2 * rows, :] = k_ref[:, cols]
        o_ref[h, 2 * rows :, :] = v_ref[:, cols]


def pack(q, k, v):
    rows, width = q.shape
    return pl.pallas_call(
        pack_body,
        out_shape=jax.ShapeDtypeStruct((width // HD, 3 * rows, HD), q.dtype),
        in_specs=[pl.BlockSpec(memory_space=pltpu.VMEM)] * 3,
        out_specs=pl.BlockSpec(memory_space=pltpu.VMEM),
        name="pack",
    )(q, k, v)


def attend_body(order, q_ref, kv_ref, o_ref, q_s, k_s, v_s):
    near, spans, xs, rows2, hd = kv_ref.shape
    rows = rows2 // 2
    q_rows = xs * rows
    k_rows = near * q_rows
    factor = 1.4426950408889634 / hd**0.5
    for r in range(spans):
        span = order[r]
        for i in range(xs):
            q_s[pl.ds(r * q_rows + i * rows, rows), :] = q_ref[span, i, 0:rows, :]
            for n in range(near):
                at = pl.ds(r * k_rows + (n * xs + i) * rows, rows)
                k_s[at, :] = kv_ref[n, span, i, 0:rows, :]
                v_s[at, :] = kv_ref[n, span, i, rows:, :]
    for r in range(spans):
        seen = (r + 1) * k_rows
        q = q_s[r * q_rows : (r + 1) * q_rows, :]
        s = lax.dot_general(
            q, k_s[0:seen, :], (((1,), (1,)), ((), ())), preferred_element_type=jnp.float32
        )
        top = jnp.max(s, axis=1, keepdims=True)
        e = jnp.exp2((s - top) * factor)
        total = jnp.sum(e, axis=1, keepdims=True)
        acc = jnp.dot(e.astype(jnp.bfloat16), v_s[0:seen, :], preferred_element_type=jnp.float32)
        out = (acc / total).astype(o_ref.dtype)
        span = order[r]
        for i in range(xs):
            o_ref[span, i] = out[i * rows : (i + 1) * rows, :]


def attend(order, q, kv):
    near, spans, xs, rows2, hd = kv.shape
    rows = rows2 // 2
    q_total = spans * xs * rows
    vmem = pl.BlockSpec(memory_space=pltpu.VMEM)
    return pl.pallas_call(
        attend_body,
        out_shape=jax.ShapeDtypeStruct((spans, xs, rows, hd), q.dtype),
        in_specs=[pl.BlockSpec(memory_space=pltpu.SMEM), vmem, vmem],
        out_specs=vmem,
        scratch_shapes=[
            pltpu.VMEM((q_total, hd), q.dtype),
            pltpu.VMEM((near * q_total, hd), q.dtype),
            pltpu.VMEM((near * q_total, hd), q.dtype),
        ],
        compiler_params=pltpu.CompilerParams(vmem_limit_bytes=40 * MIB),
        name="attend",
    )(order, q, kv)


def finish_body(level, a_ref, g_ref, o_ref):
    heads, rows, hd = a_ref.shape
    gate = g_ref[pl.ds(level[0], 1), :]
    for h in range(heads):
        cols = slice(h * hd, (h + 1) * hd)
        o_ref[:, cols] = (gate[:, cols] * a_ref[h].astype(jnp.float32)).astype(o_ref.dtype)


def finish(level, attended, gate_table):
    heads, rows, hd = attended.shape
    vmem = pl.BlockSpec(memory_space=pltpu.VMEM)
    return pl.pallas_call(
        finish_body,
        out_shape=jax.ShapeDtypeStruct((rows, heads * hd), attended.dtype),
        in_specs=[pl.BlockSpec(memory_space=pltpu.SMEM), vmem, vmem],
        out_specs=vmem,
        name="finish",
    )(level, attended, gate_table)


def local(queries, keys, values, gate_table, levels, span_rank):
    spans = span_rank.shape[0]
    places = jnp.arange(spans, dtype=jnp.int32)
    order = jnp.sum(
        jnp.where(span_rank[None, :] == places[:, None], places[None, :], 0), axis=1
    ).astype(jnp.int32)
    my_span = lax.axis_index(("yh", "z"))
    level = jnp.sum(jnp.where(places == my_span, levels, 0)).reshape(1)
    packed = pack(queries[0], keys[0], values[0])
    mine = lax.all_to_all(packed, WIDE, 0, 0, tiled=True)
    rows = queries.shape[1]
    kv = lax.all_gather(mine[:, rows:, :], NEAR, axis=0, tiled=False)
    xs = SIZES[2]
    q = mine.reshape(spans, xs, 3 * rows, HD)
    out = attend(order, q, kv.reshape(kv.shape[0], spans, xs, 2 * rows, HD))
    back = lax.all_to_all(out.reshape(spans * xs, rows, HD), WIDE, 0, 0, tiled=True)
    return finish(level, back, gate_table)[None]


def solution(mesh):
    fine = Mesh(mesh.devices.reshape(SIZES), AXES)
    split = P(("yh", "z"), ("x", "yl", "c"), None)
    return jax.shard_map(
        local,
        mesh=fine,
        in_specs=(split, split, split, P(), P(), P()),
        out_specs=split,
        check_vma=False,
    )
```

time: 561 us -> 99.6 us (0.18)
  waiting for transfers between devices: 404 us -> 35.6 us
  local copies, waits for them, and re-layouts: 86.6 us -> 3.15 us
  matrix products: 39.5 us -> 0 us
  blocking collectives: 0 us -> 26.2 us
  other arithmetic: 13.3 us -> 0.82 us
  Pallas kernels: 0 us -> 10.6 us
  starting transfers between devices: 0.04 us -> 9.39 us
    all_gather x2 -> x1, waiting for transfers between devices: 402 us -> 25.3 us  [local(): kv = lax.all_gather(mine[:, rows:, :], NEAR, axis=0, tiled=False)]
    all_gather x2 -> x0, local copies, waits for them, and re-layouts: 85.2 us -> none  [the longest x1 44.4 us: fold_call(): lax.all_gather(value_local, ('span', 'seq'), axis=0, tiled=True)]
    dot_general x2 -> x0, matrix products: 39.5 us -> none  [the longest x1 19.9 us: step(): jnp.einsum('qhd,khd->hqk', query_three, key_three, preferred_element_type...]
    all_to_all x0 -> x1, blocking collectives: none -> 26.2 us  [local(): mine = lax.all_to_all(packed, WIDE, 0, 0, tiled=True)]
    reduce_sum x4 -> x2, other arithmetic: 11.9 us -> 0.82 us  [the longest x1 0.71 us: local(): level = jnp.sum(jnp.where(places == my_span, levels, 0)).reshape(1)]
    pallas_call x0 -> x3, Pallas kernels: none -> 10.6 us  [the longest x1 5.78 us: attend(): pl.pallas_call(attend_body, out_shape=jax.ShapeDtypeStruct((spans, xs, ro...]
    all_to_all x0 -> x1, waiting for transfers between devices: none -> 10.3 us  [local(): lax.all_to_all(out.reshape(spans * xs, rows, HD), WIDE, 0, 0, tiled=True)]
    all_to_all x0 -> x1, starting transfers between devices: none -> 9.39 us  [local(): lax.all_to_all(out.reshape(spans * xs, rows, HD), WIDE, 0, 0, tiled=True)]
  transfers between devices with their start and end apart: 2 -> 2, of which waited for: 2 -> 2; matrix products, arithmetic and copies ran while one was open for 13% -> 1% of each run, Pallas kernels for 0% -> 0%
where the time goes in v1:
time: 99.6 us; the launch traced here: 99.2 us
  waiting for transfers between devices  35.6 us (36%)
  blocking collectives  26.2 us (26%)
  between operations  13.4 us (13%)
  Pallas kernels  10.6 us (11%)
  starting transfers between devices  9.39 us (9%)
  local copies, waits for them, and re-layouts  3.15 us (3%)
    all_to_all x1, blocking collectives, local(): mine = lax.all_to_all(packed, WIDE, 0, 0, tiled=True)  26.2 us
    all_gather x1, waiting for transfers between devices, local(): kv = lax.all_gather(mine[:, rows:, :], NEAR, axis=0, tiled=False)  25.3 us
    all_to_all x1, waiting for transfers between devices, local(): lax.all_to_all(out.reshape(spans * xs, rows, HD), WIDE, 0, 0, tiled=True)  10.3 us
    all_to_all x1, starting transfers between devices, local(): lax.all_to_all(out.reshape(spans * xs, rows, HD), WIDE, 0, 0, tiled=True)  9.39 us
    pallas_call x1, Pallas kernels, attend(): pl.pallas_call(attend_body, out_shape=jax.ShapeDtypeStruct((spans, xs, ro...  5.78 us
    pallas_call x1, Pallas kernels, finish(): pl.pallas_call(finish_body, out_shape=jax.ShapeDtypeStruct((rows, heads *...  2.72 us
    unnamed x8, local copies, waits for them, and re-layouts  2.29 us
    pallas_call x1, Pallas kernels, pack(): pl.pallas_call(pack_body, out_shape=jax.ShapeDtypeStruct((width // HD, 3...  2.15 us
  transfers between devices with their start and end apart: 2, of which 2 were waited for; matrix products, arithmetic and copies ran while one was open for 1% of the time, Pallas kernels for 0%

profile of v1, /device:TPU:0, one launch (start us, length us, event | category | flops | bytes accessed | tf_op | source)
XLA Modules:
  0.0 99.2 jit_solution(17614267917779903768)
XLA Ops:
  6.5 0.0 all-gather.3.cloned.1.call-start
  6.5 0.0 copy-start.2
  6.5 2.1 %pack.1 = bf16[32,96,128]{2,1,0:T(8,128)(2,1)} custom-call(bf16[32,4096]{1,0:T(8,128)(2,1)} %bitcast.10, bf16[32,4096]{1,0:T(8,128)(2,1)} %bitcast.11, bf16[32,4096]{1,0:T(8,128)(2,1)} %bitcast.12), custom_call_target="tpu_custom_call" | custom-call | tf_op jit(solution)/shard_map/pack/pallas_call | solution.py:31
  8.7 26.2 %all_to_all.10 = bf16[32,96,128]{2,1,0:T(8,128)(2,1)S(1)} all-to-all(bf16[32,96,128]{2,1,0:T(8,128)(2,1)} %pack.1), channel_id=1, replica_groups=mesh['yh'=2,'z'=4,'x'=4,'yl'=2,'c'=2] {'yh','z','x'}, dimensions={0} | all-to-all | bytes 1572864 | tf_op jit(solution)/shard_map/all_to_all | solution.py:119
  34.9 0.9 slice.4
  35.7 0.0 copy-start.3
  35.7 0.0 all-gather.3.cloned.1.call-update
  35.8 0.0 copy-done.2
  35.8 0.1 select_reduce_fusion.order
  35.9 25.3 %all-gather.3.cloned.1.call-done = bf16[128,64,128]{2,1,0:T(8,128)(2,1)} async-done(((bf16[32,64,128]{2,1,0:T(8,128)(2,1)}), bf16[128,64,128]{2,1,0:T(8,128)(2,1)}) %all-gather.3.cloned.1.call-update) | async-done | bytes 2097168 | tf_op jit(solution)/shard_map/all_gather | solution.py:121
  61.2 0.0 copy-start
  61.2 1.6 %copy-done = bf16[128,64,128]{2,1,0:T(8,128)(2,1)S(1)} copy-done((bf16[128,64,128]{2,1,0:T(8,128)(2,1)S(1)}, bf16[128,64,128]{2,1,0:T(8,128)(2,1)}, u32[]{:S(2)}) %copy-start) | copy-done | bytes 2097176
  62.8 5.8 %attend.1 = bf16[8,4,32,128]{3,2,1,0:T(8,128)(2,1)} custom-call(s32[8]{0:T(128)S(1)} %select_reduce_fusion.order, bf16[8,4,96,128]{3,2,1,0:T(8,128)(2,1)S(1)} %bitcast.8, bf16[4,8,4,64,128]{4,3,2,1,0:T(8,128)(2,1)S(1)} %bitcast.9), custom_call_target="tpu_custom_call" | custom-call | tf_op jit(solution)/shard_map/attend/pallas_call | solution.py:75
  68.6 9.4 %all-to-all-start.1 = ((bf16[32,32,128]{2,1,0:T(8,128)(2,1)}), bf16[32,32,128]{2,1,0:T(8,128)(2,1)S(1)}, u32[]{:S(2)}, u32[]{:S(2)}) async-start(bf16[32,32,128]{2,1,0:T(8,128)(2,1)} %bitcast.6), calls=%async_computation.1 | async-start | bytes 524288 | tf_op jit(solution)/shard_map/all_to_all | solution.py:125
  78.0 0.0 copy-done.3
  78.0 0.7 fusion
  78.7 10.3 %all-to-all-done.1.a_ref = bf16[32,32,128]{2,1,0:T(8,128)(2,1)S(1)} async-done(((bf16[32,32,128]{2,1,0:T(8,128)(2,1)}), bf16[32,32,128]{2,1,0:T(8,128)(2,1)S(1)}, u32[]{:S(2)}, u32[]{:S(2)}) %all-to-all-start.1) | async-done | bytes 262176 | tf_op jit(solution)/shard_map/all_to_all | solution.py:125
  89.0 0.0 copy-start.1
  89.0 0.7 copy-done.1
  89.7 2.7 %finish.1 = bf16[32,4096]{1,0:T(8,128)(2,1)} custom-call(s32[1]{0:T(128)} %bitcast.level, bf16[32,32,128]{2,1,0:T(8,128)(2,1)} %copy-done.1, f32[50,4096]{1,0:T(8,128)} %g_ref.1), custom_call_target="tpu_custom_call" | custom-call | tf_op jit(solution)/shard_map/finish/pallas_call | solution.py:101
Async XLA Ops:
  6.5 54.7 %all-gather.3.cloned.1.call-start = ((), (), s32[]{:S(2)}) async-start(), calls=%async_computation.2 | async-start | bytes 2621440 | tf_op jit(solution)/shard_map/all_gather | solution.py:121
  6.5 29.2 %copy-start.2 = (s32[8]{0:T(128)S(1)}, s32[8]{0:T(128)}, u32[]{:S(2)}) copy-start(s32[8]{0:T(128)} %param.11) | copy-start | bytes 100
  35.7 42.2 %copy-start.3 = (s32[8]{0:T(128)S(1)}, s32[8]{0:T(128)}, u32[]{:S(2)}) copy-start(s32[8]{0:T(128)} %param.10) | copy-start | bytes 100
  61.2 1.6 %copy-start = (bf16[128,64,128]{2,1,0:T(8,128)(2,1)S(1)}, bf16[128,64,128]{2,1,0:T(8,128)(2,1)}, u32[]{:S(2)}) copy-start(bf16[128,64,128]{2,1,0:T(8,128)(2,1)} %all-gather.3.cloned.1.call-done) | copy-start | bytes 6291460
  68.6 20.4 %all-to-all-start.1 = ((bf16[32,32,128]{2,1,0:T(8,128)(2,1)}), bf16[32,32,128]{2,1,0:T(8,128)(2,1)S(1)}, u32[]{:S(2)}, u32[]{:S(2)}) async-start(bf16[32,32,128]{2,1,0:T(8,128)(2,1)} %bitcast.6), calls=%async_computation.1 | async-start | bytes 524288 | tf_op jit(solution)/shard_map/all_to_all | solution.py:125
  89.0 0.7 copy-start.1
Sparse Core Ops, SparseCore 0:
  35.9 25.2 all-gather.2

commit v2 on v1

v2 whole, which is shorter than its diff:
```python
import jax
import jax.numpy as jnp
from jax import lax
from jax.experimental import pallas as pl
from jax.experimental.pallas import tpu as pltpu
from jax.sharding import Mesh
from jax.sharding import PartitionSpec as P

HD = 128
AXES = ("yh", "z", "x", "yl", "c")
SIZES = (2, 4, 4, 2, 2)
HEAD_AXES = ("yh", "z", "x")
WIDE = ("yh", "z", "x", "yl")
MIB = 1 << 20
VMEM_WHOLE = pl.BlockSpec(memory_space=pltpu.VMEM)
SMEM_WHOLE = pl.BlockSpec(memory_space=pltpu.SMEM)


def pack_body(q_ref, k_ref, v_ref, o_ref):
    rows, width = q_ref.shape
    heads = width // HD
    parts = o_ref.shape[0] // heads
    q_rows = rows // parts
    for h in range(heads):
        cols = slice(h * HD, (h + 1) * HD)
        for p in range(parts):
            to = h * parts + p
            o_ref[to, 0:q_rows, :] = q_ref[p * q_rows : (p + 1) * q_rows, cols]
            o_ref[to, q_rows : q_rows + rows, :] = k_ref[:, cols]
            o_ref[to, q_rows + rows :, :] = v_ref[:, cols]


def pack(q, k, v, parts):
    rows, width = q.shape
    return pl.pallas_call(
        pack_body,
        out_shape=jax.ShapeDtypeStruct(
            (width // HD * parts, rows // parts + 2 * rows, HD), q.dtype
        ),
        in_specs=[VMEM_WHOLE] * 3,
        out_specs=VMEM_WHOLE,
        compiler_params=pltpu.CompilerParams(vmem_limit_bytes=6 * MIB),
        name="pack",
    )(q, k, v)


def attend_body(rank, levels, head, near_ref, far_ref, gate_ref, o_ref, q_s, k_s, v_s, g_s, sem):
    spans, senders, packed, hd = near_ref.shape
    q_rows = o_ref.shape[2]
    rows = (packed - q_rows) // 2
    q_step = senders * q_rows
    k_step = 2 * senders * rows
    factor = 1.4426950408889634 / hd**0.5
    columns = pl.ds(pl.multiple_of(head[0] * hd, hd), hd)
    fetch = pltpu.make_async_copy(gate_ref.at[:, columns], g_s, sem)
    fetch.start()
    for span in range(spans):
        r = rank[span]
        q_at = pl.multiple_of(r * q_step, q_step)
        k_at = pl.multiple_of(r * k_step, k_step)
        for i in range(senders):
            q_s[pl.ds(q_at + i * q_rows, q_rows), :] = near_ref[span, i, 0:q_rows, :]
            for n, ref in enumerate((near_ref, far_ref)):
                at = pl.ds(k_at + (n * senders + i) * rows, rows)
                k_s[at, :] = ref[span, i, q_rows : q_rows + rows, :]
                v_s[at, :] = ref[span, i, q_rows + rows :, :]
    fetch.wait()
    for r in range(spans):
        span = jnp.int32(0)
        for place in range(1, spans):
            span = jnp.where(rank[place] == r, place, span)
        seen = (r + 1) * k_step
        s = lax.dot_general(
            q_s[r * q_step : (r + 1) * q_step, :],
            k_s[0:seen, :],
            (((1,), (1,)), ((), ())),
            preferred_element_type=jnp.float32,
        )
        top = jnp.max(s, axis=1, keepdims=True)
        e = jnp.exp2((s - top) * factor)
        total = jnp.sum(e, axis=1, keepdims=True)
        acc = jnp.dot(e.astype(jnp.bfloat16), v_s[0:seen, :], preferred_element_type=jnp.float32)
        attended = (acc / total).astype(jnp.bfloat16).astype(jnp.float32)
        gated = (g_s[pl.ds(levels[span], 1), :] * attended).astype(o_ref.dtype)
        for i in range(senders):
            o_ref[span, i] = gated[i * q_rows : (i + 1) * q_rows, :]


def attend(rank, levels, head, near, far, gate_table, q_rows):
    spans, senders, packed, hd = near.shape
    rows = (packed - q_rows) // 2
    q_total = spans * senders * q_rows
    k_total = 2 * spans * senders * rows
    return pl.pallas_call(
        attend_body,
        out_shape=jax.ShapeDtypeStruct((spans, senders, q_rows, hd), near.dtype),
        in_specs=[
            SMEM_WHOLE,
            SMEM_WHOLE,
            SMEM_WHOLE,
            VMEM_WHOLE,
            VMEM_WHOLE,
            pl.BlockSpec(memory_space=pl.ANY),
        ],
        out_specs=VMEM_WHOLE,
        scratch_shapes=[
            pltpu.VMEM((q_total, hd), near.dtype),
            pltpu.VMEM((k_total, hd), near.dtype),
            pltpu.VMEM((k_total, hd), near.dtype),
            pltpu.VMEM((gate_table.shape[0], hd), gate_table.dtype),
            pltpu.SemaphoreType.DMA,
        ],
        compiler_params=pltpu.CompilerParams(vmem_limit_bytes=24 * MIB),
        name="attend",
    )(rank, levels, head, near, far, gate_table)


def unpack_body(a_ref, o_ref):
    parts_heads, q_rows, hd = a_ref.shape
    parts = o_ref.shape[0] // q_rows
    for h in range(parts_heads // parts):
        for p in range(parts):
            o_ref[p * q_rows : (p + 1) * q_rows, h * hd : (h + 1) * hd] = a_ref[h * parts + p]


def unpack(a, rows):
    parts_heads, q_rows, hd = a.shape
    return pl.pallas_call(
        unpack_body,
        out_shape=jax.ShapeDtypeStruct((rows, parts_heads * q_rows // rows * hd), a.dtype),
        in_specs=[VMEM_WHOLE],
        out_specs=VMEM_WHOLE,
        compiler_params=pltpu.CompilerParams(vmem_limit_bytes=4 * MIB),
        name="unpack",
    )(a)


def local(queries, keys, values, gate_table, levels, span_rank):
    spans = span_rank.shape[0]
    rows = queries.shape[1]
    parts = SIZES[3]
    q_rows = rows // parts
    head = lax.axis_index(HEAD_AXES).astype(jnp.int32).reshape(1)
    packed = pack(queries[0], keys[0], values[0], parts)
    near = lax.all_to_all(packed, WIDE, 0, 0, tiled=True)
    far = lax.ppermute(near, "c", [(0, 1), (1, 0)])
    senders = near.shape[0] // spans
    shape = (spans, senders) + near.shape[1:]
    out = attend(
        span_rank, levels, head, near.reshape(shape), far.reshape(shape), gate_table, q_rows
    )
    back = lax.all_to_all(out.reshape(spans * senders, q_rows, HD), WIDE, 0, 0, tiled=True)
    return unpack(back, rows)[None]


def solution(mesh):
    fine = Mesh(mesh.devices.reshape(SIZES), AXES)
    split = P(("yh", "z"), ("x", "yl", "c"), None)
    return jax.shard_map(
        local,
        mesh=fine,
        in_specs=(split, split, split, P(), P(), P()),
        out_specs=split,
        check_vma=False,
    )
```

time: 99.6 us -> 61.2 us (0.61)
  waiting for transfers between devices: 35.6 us -> 3.03 us
  blocking collectives: 26.2 us -> 48.6 us
  between operations: 13.4 us -> 0.05 us
  starting transfers between devices: 9.39 us -> 0.01 us
  Pallas kernels: 10.6 us -> 6.33 us
    all_gather x1 -> x0, waiting for transfers between devices: 25.3 us -> none  [local(): kv = lax.all_gather(mine[:, rows:, :], NEAR, axis=0, tiled=False)]
    all_to_all x1 -> x2, blocking collectives: 26.2 us -> 48.6 us  [the longest x1 32.1 us: local(): near = lax.all_to_all(packed, WIDE, 0, 0, tiled=True)]
    all_to_all x1 -> x0, waiting for transfers between devices: 10.3 us -> none  [local(): lax.all_to_all(out.reshape(spans * xs, rows, HD), WIDE, 0, 0, tiled=True)]
    all_to_all x1 -> x0, starting transfers between devices: 9.39 us -> none  [local(): lax.all_to_all(out.reshape(spans * xs, rows, HD), WIDE, 0, 0, tiled=True)]
    pallas_call x3, Pallas kernels: 10.6 us -> 6.33 us  [the longest x1 5.41 us: attend(): pl.pallas_call(attend_body, out_shape=jax.ShapeDtypeStruct((spans, sender...]
    ppermute x0 -> x1, waiting for transfers between devices: none -> 3.03 us  [local(): far = lax.ppermute(near, 'c', [(0, 1), (1, 0)])]
    unnamed x8 -> x12, local copies, waits for them, and re-layouts: 2.29 us -> 2.87 us
  transfers between devices with their start and end apart: 2 -> 1, of which waited for: 2 -> 1; matrix products, arithmetic and copies ran while one was open for 1% -> 0% of each run, Pallas kernels for 0% -> 0%
where the time goes in v2:
time: 61.2 us; the launch traced here: 60.9 us
  blocking collectives  48.6 us (79%)
  Pallas kernels  6.33 us (10%)
  waiting for transfers between devices  3.03 us (5%)
  local copies, waits for them, and re-layouts  2.87 us (5%)
    all_to_all x1, blocking collectives, local(): near = lax.all_to_all(packed, WIDE, 0, 0, tiled=True)  32.1 us
    all_to_all x1, blocking collectives, local(): lax.all_to_all(out.reshape(spans * senders, q_rows, HD), WIDE, 0, 0, tile...  16.5 us
    pallas_call x1, Pallas kernels, attend(): pl.pallas_call(attend_body, out_shape=jax.ShapeDtypeStruct((spans, sender...  5.41 us
    ppermute x1, waiting for transfers between devices, local(): far = lax.ppermute(near, 'c', [(0, 1), (1, 0)])  3.03 us
    unnamed x12, local copies, waits for them, and re-layouts  2.87 us
  transfers between devices with their start and end apart: 1, of which 1 were waited for; matrix products, arithmetic and copies ran while one was open for 0% of the time, Pallas kernels for 0%

profile of v2, /device:TPU:0, one launch (start us, length us, event | category | flops | bytes accessed | tf_op | source)
XLA Modules:
  0.0 60.9 jit_solution(11983249843609131978)
XLA Ops:
  0.0 0.0 copy-start.1
  0.0 0.9 %copy-done.1 = bf16[1,32,4096]{2,1,0:T(8,128)(2,1)S(1)} copy-done((bf16[1,32,4096]{2,1,0:T(8,128)(2,1)S(1)}, bf16[1,32,4096]{2,1,0:T(8,128)(2,1)}, u32[]{:S(2)}) %copy-start.1) | copy-done | bytes 262168
  1.0 0.0 copy-start.2
  1.0 0.9 %copy-done.2 = bf16[1,32,4096]{2,1,0:T(8,128)(2,1)S(1)} copy-done((bf16[1,32,4096]{2,1,0:T(8,128)(2,1)S(1)}, bf16[1,32,4096]{2,1,0:T(8,128)(2,1)}, u32[]{:S(2)}) %copy-start.2) | copy-done | bytes 262168
  1.9 0.0 copy-start.3
  1.9 0.9 %copy-done.3 = bf16[1,32,4096]{2,1,0:T(8,128)(2,1)S(1)} copy-done((bf16[1,32,4096]{2,1,0:T(8,128)(2,1)S(1)}, bf16[1,32,4096]{2,1,0:T(8,128)(2,1)}, u32[]{:S(2)}) %copy-start.3) | copy-done | bytes 262168
  2.9 0.2 pack.1
  3.0 0.0 copy-start
  3.0 0.0 copy-start.4
  3.1 0.0 copy-start.5
  3.1 32.1 %all_to_all.10 = bf16[64,80,128]{2,1,0:T(8,128)(2,1)S(1)} all-to-all(bf16[64,80,128]{2,1,0:T(8,128)(2,1)S(1)} %pack.1), channel_id=1, replica_groups=mesh['yh'=2,'z'=4,'x'=4,'yl'=2,'c'=2] {'yh','z','x','yl'}, dimensions={0} | all-to-all | bytes 2621440 | tf_op jit(solution)/shard_map/all_to_all | solution.py:145
  35.2 0.0 collective-permute-start
  35.2 3.0 %collective-permute-done = bf16[64,80,128]{2,1,0:T(8,128)(2,1)S(1)} collective-permute-done((bf16[64,80,128]{2,1,0:T(8,128)(2,1)S(1)}, bf16[64,80,128]{2,1,0:T(8,128)(2,1)S(1)}, u32[]{:S(2)}, u32[]{:S(2)}) %collective-permute-start) | collective-permute-done | bytes 1310752 | tf_op jit(solution)/shard_map/ppermute | solution.py:146
  38.2 0.0 copy-done
  38.2 0.0 copy-done.4
  38.2 0.0 copy-done.5
  38.2 5.4 %attend.1 = bf16[8,8,16,128]{3,2,1,0:T(8,128)(2,1)S(1)} custom-call(s32[8]{0:T(128)S(1)} %copy-done.4, s32[8]{0:T(128)S(1)} %copy-done.5, s32[1]{0:T(128)} %bitcast.head, bf16[8,8,80,128]{3,2,1,0:T(8,128)(2,1)S(1)} %bitcast.8, bf16[8,8,80,128]{3,2,1,0:T(8,128)(2,1)S(1)} %bitcast.9, f32[50,4096]{1,0:T(8,128)S(1)} %copy-done), custom_call_target="tpu_custom_call" | custom-call | tf_op jit(solution)/shard_map/attend/pallas_call | solution.py:94
  43.6 16.5 %all_to_all.11.a_ref = bf16[64,16,128]{2,1,0:T(8,128)(2,1)S(1)} all-to-all(bf16[64,16,128]{2,1,0:T(8,128)(2,1)S(1)} %bitcast.10), channel_id=1, replica_groups=mesh['yh'=2,'z'=4,'x'=4,'yl'=2,'c'=2] {'yh','z','x','yl'}, dimensions={0} | all-to-all | bytes 524288 | tf_op jit(solution)/shard_map/all_to_all | solution.py:152
  60.2 0.7 %unpack.1 = bf16[32,4096]{1,0:T(8,128)(2,1)} custom-call(bf16[64,16,128]{2,1,0:T(8,128)(2,1)S(1)} %all_to_all.11.a_ref), custom_call_target="tpu_custom_call" | custom-call | tf_op jit(solution)/shard_map/unpack/pallas_call | solution.py:128
Async XLA Ops:
  0.0 0.9 %copy-start.1 = (bf16[1,32,4096]{2,1,0:T(8,128)(2,1)S(1)}, bf16[1,32,4096]{2,1,0:T(8,128)(2,1)}, u32[]{:S(2)}) copy-start(bf16[1,32,4096]{2,1,0:T(8,128)(2,1)} %param.6) | copy-start | bytes 786436
  1.0 0.9 %copy-start.2 = (bf16[1,32,4096]{2,1,0:T(8,128)(2,1)S(1)}, bf16[1,32,4096]{2,1,0:T(8,128)(2,1)}, u32[]{:S(2)}) copy-start(bf16[1,32,4096]{2,1,0:T(8,128)(2,1)} %param.7) | copy-start | bytes 786436
  1.9 0.9 %copy-start.3 = (bf16[1,32,4096]{2,1,0:T(8,128)(2,1)S(1)}, bf16[1,32,4096]{2,1,0:T(8,128)(2,1)}, u32[]{:S(2)}) copy-start(bf16[1,32,4096]{2,1,0:T(8,128)(2,1)} %param.8) | copy-start | bytes 786436
  3.0 35.2 %copy-start = (f32[50,4096]{1,0:T(8,128)S(1)}, f32[50,4096]{1,0:T(8,128)}, u32[]{:S(2)}) copy-start(f32[50,4096]{1,0:T(8,128)} %gate_ref.1) | copy-start | bytes 2457604
  3.0 35.2 %copy-start.4 = (s32[8]{0:T(128)S(1)}, s32[8]{0:T(128)}, u32[]{:S(2)}) copy-start(s32[8]{0:T(128)} %rank.1) | copy-start | bytes 100
  3.1 35.2 %copy-start.5 = (s32[8]{0:T(128)S(1)}, s32[8]{0:T(128)}, u32[]{:S(2)}) copy-start(s32[8]{0:T(128)} %levels.1) | copy-start | bytes 100
  35.2 3.0 %collective-permute-start = (bf16[64,80,128]{2,1,0:T(8,128)(2,1)S(1)}, bf16[64,80,128]{2,1,0:T(8,128)(2,1)S(1)}, u32[]{:S(2)}, u32[]{:S(2)}) collective-permute-start(bf16[64,80,128]{2,1,0:T(8,128)(2,1)S(1)} %all_to_all.10), channel_id=1, source_target_pairs={{0,1},{1,0},{2,3},{3,2},{4,5},{5,4},{6,7},{7,6},{8,9},{9,8},{10,11... | collective-permute-start | bytes 3932168 | tf_op jit(solution)/shard_map/ppermute | solution.py:146

commit v3 on v2

v3 whole, which is shorter than its diff:
```python
import jax
import jax.numpy as jnp
from jax import lax
from jax.experimental import pallas as pl
from jax.experimental.pallas import tpu as pltpu
from jax.sharding import Mesh
from jax.sharding import PartitionSpec as P

HD = 128
AXES = ("yh", "z", "x", "yl", "c")
SIZES = (2, 4, 4, 2, 2)
HEAD_AXES = ("yh", "z", "x")
WIDE = ("yh", "z", "x", "yl")
LOG2E = 1.4426950408889634
STAT = 8
MIB = 1 << 20
VMEM_WHOLE = pl.BlockSpec(memory_space=pltpu.VMEM)
SMEM_WHOLE = pl.BlockSpec(memory_space=pltpu.SMEM)
ANYWHERE = pl.BlockSpec(memory_space=pl.ANY)


def pack_body(q_any, k_any, v_any, o_ref, q_ref, k_ref, v_ref, sems):
    copies = [
        pltpu.make_async_copy(src, dst, sems.at[i])
        for i, (src, dst) in enumerate(((q_any, q_ref), (k_any, k_ref), (v_any, v_ref)))
    ]
    for copy in copies:
        copy.start()
    rows, width = q_ref.shape
    heads = width // HD
    parts = o_ref.shape[0] // heads
    k_rows = rows // parts
    copies[0].wait()
    for h in range(heads):
        block = q_ref[:, h * HD : (h + 1) * HD]
        for p in range(parts):
            o_ref[h * parts + p, 0:rows, :] = block
    for n, ref in enumerate((k_ref, v_ref)):
        copies[n + 1].wait()
        for h in range(heads):
            for p in range(parts):
                o_ref[h * parts + p, rows + n * k_rows : rows + (n + 1) * k_rows, :] = ref[
                    p * k_rows : (p + 1) * k_rows, h * HD : (h + 1) * HD
                ]


def pack(q, k, v, parts):
    rows, width = q.shape
    return pl.pallas_call(
        pack_body,
        out_shape=jax.ShapeDtypeStruct(
            (width // HD * parts, rows + 2 * (rows // parts), HD), q.dtype
        ),
        in_specs=[ANYWHERE] * 3,
        out_specs=VMEM_WHOLE,
        scratch_shapes=[pltpu.VMEM((rows, width), q.dtype)] * 3
        + [pltpu.SemaphoreType.DMA((3,))],
        compiler_params=pltpu.CompilerParams(vmem_limit_bytes=6 * MIB),
        name="pack",
    )(q, k, v)


def attend_body(rank, levels, head, near_ref, far_ref, gate_ref, o_ref, q_s, k_s, v_s, g_s, sem):
    spans, senders, packed, hd = near_ref.shape
    rows = o_ref.shape[2] - STAT
    k_rows = (packed - rows) // 2
    q_step = senders * rows
    k_step = 2 * senders * k_rows
    factor = LOG2E / hd**0.5
    columns = pl.ds(pl.multiple_of(head[0] * hd, hd), hd)
    fetch = pltpu.make_async_copy(gate_ref.at[:, columns], g_s, sem)
    fetch.start()
    for span in range(spans):
        r = rank[span]
        q_at = pl.multiple_of(r * q_step, q_step)
        k_at = pl.multiple_of(r * k_step, k_step)
        for i in range(senders):
            q_s[pl.ds(q_at + i * rows, rows), :] = near_ref[span, i, 0:rows, :]
            for n, ref in enumerate((near_ref, far_ref)):
                at = pl.ds(k_at + (n * senders + i) * k_rows, k_rows)
                k_s[at, :] = ref[span, i, rows : rows + k_rows, :]
                v_s[at, :] = ref[span, i, rows + k_rows :, :]
    fetch.wait()
    diagonal = lax.broadcasted_iota(jnp.int32, (hd, hd), 0) == lax.broadcasted_iota(
        jnp.int32, (hd, hd), 1
    )
    for r in range(spans):
        span = jnp.int32(0)
        for place in range(1, spans):
            span = jnp.where(rank[place] == r, place, span)
        seen = (r + 1) * k_step
        s = lax.dot_general(
            q_s[r * q_step : (r + 1) * q_step, :],
            k_s[0:seen, :],
            (((1,), (1,)), ((), ())),
            preferred_element_type=jnp.float32,
        )
        top = jnp.max(s, axis=1, keepdims=True)
        e = jnp.exp2((s - top) * factor)
        total = jnp.sum(e, axis=1, keepdims=True)
        acc = jnp.dot(e.astype(jnp.bfloat16), v_s[0:seen, :], preferred_element_type=jnp.float32)
        gated = (g_s[pl.ds(levels[span], 1), :] * (acc / total)).astype(o_ref.dtype)
        logs = top * factor + jnp.log2(total)
        for i in range(senders):
            o_ref[span, i, 0:rows, :] = gated[i * rows : (i + 1) * rows, :]
        for j in range(q_step // hd):
            line = jnp.sum(
                jnp.where(diagonal, logs[j * hd : (j + 1) * hd, :], 0.0), axis=0, keepdims=True
            )
            high = line.astype(jnp.bfloat16).astype(jnp.float32)
            middle = (line - high).astype(jnp.bfloat16).astype(jnp.float32)
            low = line - high - middle
            stat = jnp.concatenate(
                [high, middle, low, jnp.zeros((STAT - 3, hd), jnp.float32)], axis=0
            ).astype(o_ref.dtype)
            for i in range(j * hd // rows, (j + 1) * hd // rows):
                o_ref[span, i, rows : rows + STAT, :] = stat


def attend(rank, levels, head, near, far, gate_table, rows):
    spans, senders, packed, hd = near.shape
    q_total = spans * senders * rows
    k_total = spans * senders * (packed - rows)
    return pl.pallas_call(
        attend_body,
        out_shape=jax.ShapeDtypeStruct((spans, senders, rows + STAT, hd), near.dtype),
        in_specs=[SMEM_WHOLE, SMEM_WHOLE, SMEM_WHOLE, VMEM_WHOLE, VMEM_WHOLE, ANYWHERE],
        out_specs=VMEM_WHOLE,
        scratch_shapes=[
            pltpu.VMEM((q_total, hd), near.dtype),
            pltpu.VMEM((k_total, hd), near.dtype),
            pltpu.VMEM((k_total, hd), near.dtype),
            pltpu.VMEM((gate_table.shape[0], hd), gate_table.dtype),
            pltpu.SemaphoreType.DMA,
        ],
        compiler_params=pltpu.CompilerParams(vmem_limit_bytes=24 * MIB),
        name="attend",
    )(rank, levels, head, near, far, gate_table)


def join_body(place, a_ref, o_ref, w_s):
    heads, _, packed, hd = a_ref.shape
    rows = packed - STAT
    logs = [
        jnp.sum(a_ref[:, p, rows:packed, :].astype(jnp.float32), axis=1) for p in range(2)
    ]
    share = 1.0 / (1.0 + jnp.exp2(logs[1] - logs[0]))
    w_s[...] = share.T
    mine = w_s[pl.ds(pl.multiple_of(place[0] * rows, rows), rows), :]
    for h in range(heads):
        first = a_ref[h, 0, 0:rows, :].astype(jnp.float32)
        second = a_ref[h, 1, 0:rows, :].astype(jnp.float32)
        w = mine[:, h : h + 1]
        joined = w * first + (1.0 - w) * second
        o_ref[:, h * hd : (h + 1) * hd] = joined.astype(o_ref.dtype)


def join(place, a):
    heads, _, packed, hd = a.shape
    return pl.pallas_call(
        join_body,
        out_shape=jax.ShapeDtypeStruct((packed - STAT, heads * hd), a.dtype),
        in_specs=[SMEM_WHOLE, VMEM_WHOLE],
        out_specs=VMEM_WHOLE,
        scratch_shapes=[pltpu.VMEM((hd, heads), jnp.float32)],
        compiler_params=pltpu.CompilerParams(vmem_limit_bytes=4 * MIB),
        name="join",
    )(place, a)


def local(queries, keys, values, gate_table, levels, span_rank):
    spans = span_rank.shape[0]
    rows = queries.shape[1]
    parts = SIZES[3]
    head = lax.axis_index(HEAD_AXES).astype(jnp.int32).reshape(1)
    place = lax.rem(lax.axis_index(("x", "yl")), HD // rows).astype(jnp.int32).reshape(1)
    packed = pack(queries[0], keys[0], values[0], parts)
    near = lax.all_to_all(packed, WIDE, 0, 0, tiled=True)
    far = lax.ppermute(near, "c", [(0, 1), (1, 0)])
    senders = near.shape[0] // spans
    shape = (spans, senders) + near.shape[1:]
    out = attend(
        span_rank, levels, head, near.reshape(shape), far.reshape(shape), gate_table, rows
    )
    back = lax.all_to_all(
        out.reshape(spans * senders, rows + STAT, HD), WIDE, 0, 0, tiled=True
    )
    return join(place, back.reshape(-1, parts, rows + STAT, HD))[None]


def solution(mesh):
    fine = Mesh(mesh.devices.reshape(SIZES), AXES)
    split = P(("yh", "z"), ("x", "yl", "c"), None)
    return jax.shard_map(
        local,
        mesh=fine,
        in_specs=(split, split, split, P(), P(), P()),
        out_specs=split,
        check_vma=False,
    )
```

time: 61.2 us -> 64.3 us (1.051)
  blocking collectives: 48.6 us -> 29.5 us
  waiting for transfers between devices: 3.03 us -> 17.2 us
  starting transfers between devices: 0.01 us -> 5.83 us
  Pallas kernels: 6.33 us -> 7.88 us
  local copies, waits for them, and re-layouts: 2.87 us -> 3.52 us
    all_to_all x1 -> x0, blocking collectives: 16.5 us -> none  [local(): lax.all_to_all(out.reshape(spans * senders, q_rows, HD), WIDE, 0, 0, tile...]
    all_to_all x0 -> x1, waiting for transfers between devices: none -> 14.5 us  [local(): lax.all_to_all(out.reshape(spans * senders, rows + STAT, HD), WIDE, 0, 0,...]
    all_to_all x0 -> x1, starting transfers between devices: none -> 5.82 us  [local(): lax.all_to_all(out.reshape(spans * senders, rows + STAT, HD), WIDE, 0, 0,...]
    all_to_all x1, blocking collectives: 32.1 us -> 29.5 us  [local(): near = lax.all_to_all(packed, WIDE, 0, 0, tiled=True)]
    pallas_call x1, Pallas kernels: 5.41 us -> 6.33 us  [attend(): pl.pallas_call(attend_body, out_shape=jax.ShapeDtypeStruct((spans, sender...]
    unnamed x12, local copies, waits for them, and re-layouts: 2.87 us -> 3.52 us
  transfers between devices with their start and end apart: 1 -> 2, of which waited for: 1 -> 2; matrix products, arithmetic and copies ran while one was open for 0% -> 0% of each run, Pallas kernels for 0% -> 0%
where the time goes in v3:
time: 64.3 us; the launch traced here: 64 us
  blocking collectives  29.5 us (46%)
  waiting for transfers between devices  17.2 us (27%)
  Pallas kernels  7.88 us (12%)
  starting transfers between devices  5.83 us (9%)
  local copies, waits for them, and re-layouts  3.52 us (5%)
    all_to_all x1, blocking collectives, local(): near = lax.all_to_all(packed, WIDE, 0, 0, tiled=True)  29.5 us
    all_to_all x1, waiting for transfers between devices, local(): lax.all_to_all(out.reshape(spans * senders, rows + STAT, HD), WIDE, 0, 0,...  14.5 us
    pallas_call x1, Pallas kernels, attend(): pl.pallas_call(attend_body, out_shape=jax.ShapeDtypeStruct((spans, sender...  6.33 us
    all_to_all x1, starting transfers between devices, local(): lax.all_to_all(out.reshape(spans * senders, rows + STAT, HD), WIDE, 0, 0,...  5.82 us
    unnamed x12, local copies, waits for them, and re-layouts  3.52 us
    ppermute x1, waiting for transfers between devices, local(): far = lax.ppermute(near, 'c', [(0, 1), (1, 0)])  2.66 us
    pallas_call x1, Pallas kernels, join(): pl.pallas_call(join_body, out_shape=jax.ShapeDtypeStruct((packed - STAT,...  1.31 us
  transfers between devices with their start and end apart: 2, of which 2 were waited for; matrix products, arithmetic and copies ran while one was open for 0% of the time, Pallas kernels for 0%

profile of v3, /device:TPU:0, one launch (start us, length us, event | category | flops | bytes accessed | tf_op | source)
XLA Modules:
  0.0 64.0 jit_solution(10287633371755637255)
XLA Ops:
  0.0 0.0 copy-start.1
  0.0 0.9 %copy-done.1 = bf16[1,32,4096]{2,1,0:T(8,128)(2,1)S(1)} copy-done((bf16[1,32,4096]{2,1,0:T(8,128)(2,1)S(1)}, bf16[1,32,4096]{2,1,0:T(8,128)(2,1)}, u32[]{:S(2)}) %copy-start.1) | copy-done | bytes 262168
  1.0 0.0 copy-start.2
  1.0 0.9 %copy-done.2 = bf16[1,32,4096]{2,1,0:T(8,128)(2,1)S(1)} copy-done((bf16[1,32,4096]{2,1,0:T(8,128)(2,1)S(1)}, bf16[1,32,4096]{2,1,0:T(8,128)(2,1)}, u32[]{:S(2)}) %copy-start.2) | copy-done | bytes 262168
  1.9 0.0 copy-start.3
  1.9 0.9 %copy-done.3 = bf16[1,32,4096]{2,1,0:T(8,128)(2,1)S(1)} copy-done((bf16[1,32,4096]{2,1,0:T(8,128)(2,1)S(1)}, bf16[1,32,4096]{2,1,0:T(8,128)(2,1)}, u32[]{:S(2)}) %copy-start.3) | copy-done | bytes 262168
  2.9 0.2 pack.1
  3.1 0.0 copy-start
  3.1 29.5 %all_to_all.10 = bf16[64,64,128]{2,1,0:T(8,128)(2,1)S(1)} all-to-all(bf16[64,64,128]{2,1,0:T(8,128)(2,1)S(1)} %pack.1), channel_id=1, replica_groups=mesh['yh'=2,'z'=4,'x'=4,'yl'=2,'c'=2] {'yh','z','x','yl'}, dimensions={0} | all-to-all | bytes 2097152 | tf_op jit(solution)/shard_map/all_to_all | solution.py:178
  32.7 0.0 collective-permute-start
  32.7 2.7 %collective-permute-done = bf16[64,64,128]{2,1,0:T(8,128)(2,1)S(1)} collective-permute-done((bf16[64,64,128]{2,1,0:T(8,128)(2,1)S(1)}, bf16[64,64,128]{2,1,0:T(8,128)(2,1)S(1)}, u32[]{:S(2)}, u32[]{:S(2)}) %collective-permute-start) | collective-permute-done | bytes 1048608 | tf_op jit(solution)/shard_map/ppermute | solution.py:179
  35.3 0.0 copy-start.4
  35.3 0.0 copy-start.5
  35.3 0.0 copy-done
  35.3 0.6 %copy-done.4 = s32[8]{0:T(128)S(1)} copy-done((s32[8]{0:T(128)S(1)}, s32[8]{0:T(128)}, u32[]{:S(2)}) %copy-start.4) | copy-done | bytes 56
  36.0 0.0 copy-done.5
  36.0 6.3 %attend.1 = bf16[8,8,40,128]{3,2,1,0:T(8,128)(2,1)} custom-call(s32[8]{0:T(128)S(1)} %copy-done.4, s32[8]{0:T(128)S(1)} %copy-done.5, s32[1]{0:T(128)} %bitcast.1.head, bf16[8,8,64,128]{3,2,1,0:T(8,128)(2,1)S(1)} %bitcast.10, bf16[8,8,64,128]{3,2,1,0:T(8,128)(2,1)S(1)} %bitcast.12, f32[50,4096]{1,0:T(8,128)S(1)} %copy-done), custom_call_target="tpu_custom_call" | custom-call | tf_op jit(solution)/shard_map/attend/pallas_call | solution.py:124
  42.3 5.8 %all-to-all-start.1 = ((bf16[64,40,128]{2,1,0:T(8,128)(2,1)}), bf16[64,40,128]{2,1,0:T(8,128)(2,1)S(1)}, u32[]{:S(2)}, u32[]{:S(2)}) async-start(bf16[64,40,128]{2,1,0:T(8,128)(2,1)} %bitcast.7), calls=%async_computation.1 | async-start | bytes 1310720 | tf_op jit(solution)/shard_map/all_to_all | solution.py:185
  48.2 14.5 %all-to-all-done.1 = bf16[64,40,128]{2,1,0:T(8,128)(2,1)S(1)} async-done(((bf16[64,40,128]{2,1,0:T(8,128)(2,1)}), bf16[64,40,128]{2,1,0:T(8,128)(2,1)S(1)}, u32[]{:S(2)}, u32[]{:S(2)}) %all-to-all-start.1) | async-done | bytes 655392 | tf_op jit(solution)/shard_map/all_to_all | solution.py:185
  62.7 1.3 %join.1 = bf16[32,4096]{1,0:T(8,128)(2,1)} custom-call(s32[1]{0:T(128)} %bitcast.place, bf16[32,2,40,128]{3,2,1,0:T(8,128)(2,1)S(1)} %bitcast.11), custom_call_target="tpu_custom_call" | custom-call | tf_op jit(solution)/shard_map/join/pallas_call | solution.py:160
Async XLA Ops:
  0.0 0.9 %copy-start.1 = (bf16[1,32,4096]{2,1,0:T(8,128)(2,1)S(1)}, bf16[1,32,4096]{2,1,0:T(8,128)(2,1)}, u32[]{:S(2)}) copy-start(bf16[1,32,4096]{2,1,0:T(8,128)(2,1)} %param.6) | copy-start | bytes 786436
  1.0 0.9 %copy-start.2 = (bf16[1,32,4096]{2,1,0:T(8,128)(2,1)S(1)}, bf16[1,32,4096]{2,1,0:T(8,128)(2,1)}, u32[]{:S(2)}) copy-start(bf16[1,32,4096]{2,1,0:T(8,128)(2,1)} %param.7) | copy-start | bytes 786436
  1.9 0.9 %copy-start.3 = (bf16[1,32,4096]{2,1,0:T(8,128)(2,1)S(1)}, bf16[1,32,4096]{2,1,0:T(8,128)(2,1)}, u32[]{:S(2)}) copy-start(bf16[1,32,4096]{2,1,0:T(8,128)(2,1)} %param.8) | copy-start | bytes 786436
  3.1 32.2 %copy-start = (f32[50,4096]{1,0:T(8,128)S(1)}, f32[50,4096]{1,0:T(8,128)}, u32[]{:S(2)}) copy-start(f32[50,4096]{1,0:T(8,128)} %gate_ref.1) | copy-start | bytes 2457604
  32.7 2.7 %collective-permute-start = (bf16[64,64,128]{2,1,0:T(8,128)(2,1)S(1)}, bf16[64,64,128]{2,1,0:T(8,128)(2,1)S(1)}, u32[]{:S(2)}, u32[]{:S(2)}) collective-permute-start(bf16[64,64,128]{2,1,0:T(8,128)(2,1)S(1)} %all_to_all.10), channel_id=1, source_target_pairs={{0,1},{1,0},{2,3},{3,2},{4,5},{5,4},{6,7},{7,6},{8,9},{9,8},{10,11... | collective-permute-start | bytes 3145736 | tf_op jit(solution)/shard_map/ppermute | solution.py:179
  35.3 0.7 %copy-start.4 = (s32[8]{0:T(128)S(1)}, s32[8]{0:T(128)}, u32[]{:S(2)}) copy-start(s32[8]{0:T(128)} %rank.1) | copy-start | bytes 100
  35.3 0.7 %copy-start.5 = (s32[8]{0:T(128)S(1)}, s32[8]{0:T(128)}, u32[]{:S(2)}) copy-start(s32[8]{0:T(128)} %levels.1) | copy-start | bytes 100
  42.3 20.3 %all-to-all-start.1 = ((bf16[64,40,128]{2,1,0:T(8,128)(2,1)}), bf16[64,40,128]{2,1,0:T(8,128)(2,1)S(1)}, u32[]{:S(2)}, u32[]{:S(2)}) async-start(bf16[64,40,128]{2,1,0:T(8,128)(2,1)} %bitcast.7), calls=%async_computation.1 | async-start | bytes 1310720 | tf_op jit(solution)/shard_map/all_to_all | solution.py:185

commit v4 on v2

v4 whole, which is shorter than its diff:
```python
import functools

import jax
import jax.numpy as jnp
from jax import lax
from jax.experimental import pallas as pl
from jax.experimental.pallas import tpu as pltpu
from jax.sharding import Mesh
from jax.sharding import PartitionSpec as P

HD = 128
AXES = ("yh", "z", "x", "yl", "c")
SIZES = (2, 4, 4, 2, 2)
HEAD_AXES = ("yh", "z", "x")
WIDE = ("yh", "z", "x", "yl")
MIB = 1 << 20
VMEM_WHOLE = pl.BlockSpec(memory_space=pltpu.VMEM)
SMEM_WHOLE = pl.BlockSpec(memory_space=pltpu.SMEM)
HBM_WHOLE = pl.BlockSpec(memory_space=pltpu.HBM)
LOG2E = 1.4426950408889634
ROW_BY_ROW = (((1,), (1,)), ((), ()))


def pack_body(q_hbm, k_hbm, v_hbm, o_ref, q_ref, k_ref, v_ref, sems):
    copies = [
        pltpu.make_async_copy(src, dst, sems.at[i])
        for i, (src, dst) in enumerate(((q_hbm, q_ref), (k_hbm, k_ref), (v_hbm, v_ref)))
    ]
    for copy in copies:
        copy.start()
    rows, width = q_ref.shape
    heads = width // HD
    parts = o_ref.shape[0] // heads
    q_rows = rows // parts
    copies[0].wait()
    for h in range(heads):
        for p in range(parts):
            o_ref[h * parts + p, 0:q_rows, :] = q_ref[
                p * q_rows : (p + 1) * q_rows, h * HD : (h + 1) * HD
            ]
    for n, ref in enumerate((k_ref, v_ref)):
        copies[n + 1].wait()
        for h in range(heads):
            block = ref[:, h * HD : (h + 1) * HD]
            for p in range(parts):
                o_ref[h * parts + p, q_rows + n * rows : q_rows + (n + 1) * rows, :] = block


def pack(q, k, v, parts):
    rows, width = q.shape
    return pl.pallas_call(
        pack_body,
        out_shape=jax.ShapeDtypeStruct(
            (width // HD * parts, rows // parts + 2 * rows, HD), q.dtype
        ),
        in_specs=[HBM_WHOLE] * 3,
        out_specs=VMEM_WHOLE,
        scratch_shapes=[pltpu.VMEM((rows, width), q.dtype)] * 3
        + [pltpu.SemaphoreType.DMA((3,))],
        compiler_params=pltpu.CompilerParams(vmem_limit_bytes=6 * MIB),
        name="pack",
    )(*(pltpu.with_memory_space_constraint(a, pltpu.HBM) for a in (q, k, v)))


def span_order(rank, spans):
    order = []
    for place in range(spans):
        span = jnp.int32(0)
        for s in range(1, spans):
            span = jnp.where(rank[s] == place, s, span)
        order.append(span)
    return order


def score_visible(order, q_ref, kv_ref, q_rows, q_s, s_s):
    spans, senders, packed, hd = kv_ref.shape
    rows = (packed - q_rows) // 2
    q_step, k_step = senders * q_rows, senders * rows
    for r in range(spans):
        q_s[r * q_step : (r + 1) * q_step, :] = q_ref[order[r], :, 0:q_rows, :].reshape(q_step, hd)
    for b in range(spans):
        k = kv_ref[order[b], :, q_rows : q_rows + rows, :].reshape(k_step, hd)
        s_s[b * q_step :, b * k_step : (b + 1) * k_step] = lax.dot_general(
            q_s[b * q_step :, :], k, ROW_BY_ROW, preferred_element_type=jnp.float32
        )


def weighted_values(order, g, group, kv_ref, q_rows, p_s):
    spans, senders, packed, hd = kv_ref.shape
    rows = (packed - q_rows) // 2
    q_step, k_step = senders * q_rows, senders * rows
    for a in range(group - 1):
        r = g * group + a
        p_s[r * q_step : (r + 1) * q_step, (r + 1) * k_step : (g + 1) * group * k_step] = jnp.zeros(
            (q_step, (group - 1 - a) * k_step), p_s.dtype
        )
    acc = None
    for b in range((g + 1) * group):
        v = kv_ref[order[b], :, q_rows + rows :, :].reshape(k_step, hd)
        part = jnp.dot(
            p_s[g * group * q_step : (g + 1) * group * q_step, b * k_step : (b + 1) * k_step],
            v,
            preferred_element_type=jnp.float32,
        )
        acc = part if acc is None else acc + part
    return acc


def near_body(q_rows, rank, near_ref, acc_ref, top_ref, total_ref, q_s, s_s, p_s):
    spans, senders, packed, hd = near_ref.shape
    q_step, k_step = senders * q_rows, senders * (packed - q_rows) // 2
    factor = LOG2E / hd**0.5
    order = span_order(rank, spans)
    score_visible(order, near_ref, near_ref, q_rows, q_s, s_s)
    for r in range(spans):
        here = slice(r * q_step, (r + 1) * q_step)
        s = s_s[here, 0 : (r + 1) * k_step]
        top = jnp.max(s, axis=1, keepdims=True)
        e = jnp.exp2((s - top) * factor)
        top_ref[here, :] = top
        total_ref[here, :] = jnp.sum(e, axis=1, keepdims=True)
        p_s[here, 0 : (r + 1) * k_step] = e.astype(p_s.dtype)
    for g in range(spans // 2):
        acc_ref[2 * g * q_step : 2 * (g + 1) * q_step, :] = weighted_values(
            order, g, 2, near_ref, q_rows, p_s
        )


def far_body(
    q_rows, rank, levels, head, near_ref, far_ref, acc_ref, top_ref, total_ref, gate_ref,
    o_ref, q_s, s_s, p_s, g_s, scale_s, total_s, sem,
):
    spans, senders, packed, hd = near_ref.shape
    q_step, k_step = senders * q_rows, senders * (packed - q_rows) // 2
    factor = LOG2E / hd**0.5
    columns = pl.ds(pl.multiple_of(head[0] * hd, hd), hd)
    fetch = pltpu.make_async_copy(gate_ref.at[:, columns], g_s, sem)
    fetch.start()
    order = span_order(rank, spans)
    score_visible(order, near_ref, far_ref, q_rows, q_s, s_s)
    for r in range(spans):
        here = slice(r * q_step, (r + 1) * q_step)
        s = s_s[here, 0 : (r + 1) * k_step]
        top = jnp.maximum(jnp.max(s, axis=1, keepdims=True), top_ref[here, :])
        e = jnp.exp2((s - top) * factor)
        scale = jnp.exp2((top_ref[here, :] - top) * factor)
        scale_s[here, :] = scale
        total_s[here, :] = total_ref[here, :] * scale + jnp.sum(e, axis=1, keepdims=True)
        p_s[here, 0 : (r + 1) * k_step] = e.astype(p_s.dtype)
    fetch.wait()
    for g in range(spans // 2):
        acc = weighted_values(order, g, 2, far_ref, q_rows, p_s)
        for a in range(2):
            r = 2 * g + a
            here = slice(r * q_step, (r + 1) * q_step)
            both = acc_ref[here, :] * scale_s[here, :] + acc[a * q_step : (a + 1) * q_step, :]
            attended = (both / total_s[here, :]).astype(jnp.bfloat16).astype(jnp.float32)
            gated = (g_s[pl.ds(levels[order[r]], 1), :] * attended).astype(o_ref.dtype)
            o_ref[order[r]] = gated.reshape(senders, q_rows, hd)


def attend_scratch(spans, senders, q_rows, rows, hd, dtype):
    q_total, k_total = spans * senders * q_rows, spans * senders * rows
    return [
        pltpu.VMEM((q_total, hd), dtype),
        pltpu.VMEM((q_total, k_total), jnp.float32),
        pltpu.VMEM((q_total, k_total), dtype),
    ]


def attend_near(rank, near, q_rows):
    spans, senders, packed, hd = near.shape
    rows = (packed - q_rows) // 2
    q_total, k_total = spans * senders * q_rows, spans * senders * rows
    return pl.pallas_call(
        functools.partial(near_body, q_rows),
        out_shape=(
            jax.ShapeDtypeStruct((q_total, hd), jnp.float32),
            jax.ShapeDtypeStruct((q_total, 1), jnp.float32),
            jax.ShapeDtypeStruct((q_total, 1), jnp.float32),
        ),
        in_specs=[SMEM_WHOLE, VMEM_WHOLE],
        out_specs=(VMEM_WHOLE,) * 3,
        scratch_shapes=attend_scratch(spans, senders, q_rows, rows, hd, near.dtype),
        compiler_params=pltpu.CompilerParams(vmem_limit_bytes=24 * MIB),
        cost_estimate=pl.CostEstimate(
            flops=4 * q_total * k_total * hd, bytes_accessed=8 * MIB, transcendentals=0
        ),
        name="attend_near",
    )(rank, near)


def attend_far(rank, levels, head, near, far, acc, top, total, gate_table, q_rows):
    spans, senders, packed, hd = near.shape
    rows = (packed - q_rows) // 2
    q_total = spans * senders * q_rows
    return pl.pallas_call(
        functools.partial(far_body, q_rows),
        out_shape=jax.ShapeDtypeStruct((spans, senders, q_rows, hd), near.dtype),
        in_specs=[SMEM_WHOLE] * 3 + [VMEM_WHOLE] * 5 + [HBM_WHOLE],
        out_specs=VMEM_WHOLE,
        scratch_shapes=attend_scratch(spans, senders, q_rows, rows, hd, near.dtype)
        + [
            pltpu.VMEM((gate_table.shape[0], hd), gate_table.dtype),
            pltpu.VMEM((q_total, 1), jnp.float32),
            pltpu.VMEM((q_total, 1), jnp.float32),
            pltpu.SemaphoreType.DMA,
        ],
        compiler_params=pltpu.CompilerParams(vmem_limit_bytes=24 * MIB),
        name="attend_far",
    )(rank, levels, head, near, far, acc, top, total, gate_table)


def unpack_body(a_ref, o_ref):
    parts_heads, q_rows, hd = a_ref.shape
    parts = o_ref.shape[0] // q_rows
    for h in range(parts_heads // parts):
        for p in range(parts):
            o_ref[p * q_rows : (p + 1) * q_rows, h * hd : (h + 1) * hd] = a_ref[h * parts + p]


def unpack(a, rows):
    parts_heads, q_rows, hd = a.shape
    return pl.pallas_call(
        unpack_body,
        out_shape=jax.ShapeDtypeStruct((rows, parts_heads * q_rows // rows * hd), a.dtype),
        in_specs=[VMEM_WHOLE],
        out_specs=VMEM_WHOLE,
        compiler_params=pltpu.CompilerParams(vmem_limit_bytes=4 * MIB),
        name="unpack",
    )(a)


def local(queries, keys, values, gate_table, levels, span_rank):
    spans = span_rank.shape[0]
    rows = queries.shape[1]
    parts = SIZES[3]
    q_rows = rows // parts
    head = lax.axis_index(HEAD_AXES).astype(jnp.int32).reshape(1)
    packed = pack(queries[0], keys[0], values[0], parts)
    near = lax.all_to_all(packed, WIDE, 0, 0, tiled=True)
    far = lax.ppermute(near, "c", [(0, 1), (1, 0)])
    senders = near.shape[0] // spans
    shape = (spans, senders) + near.shape[1:]
    near, far = near.reshape(shape), far.reshape(shape)
    part = attend_near(span_rank, near, q_rows)
    out = attend_far(span_rank, levels, head, near, far, *part, gate_table, q_rows)
    back = lax.all_to_all(out.reshape(spans * senders, q_rows, HD), WIDE, 0, 0, tiled=True)
    return unpack(back, rows)[None]


def solution(mesh):
    fine = Mesh(mesh.devices.reshape(SIZES), AXES)
    split = P(("yh", "z"), ("x", "yl", "c"), None)
    return jax.shard_map(
        local,
        mesh=fine,
        in_specs=(split, split, split, P(), P(), P()),
        out_specs=split,
        check_vma=False,
    )
```

time: 61.2 us -> 56.9 us (0.930)
  local copies, waits for them, and re-layouts: 2.87 us -> 0.02 us
  waiting for transfers between devices: 3.03 us -> 0.56 us
  Pallas kernels: 6.33 us -> 7.59 us
    unnamed x12 -> x6, local copies, waits for them, and re-layouts: 2.87 us -> 0.02 us
    ppermute x1, waiting for transfers between devices: 3.03 us -> 0.56 us  [local(): far = lax.ppermute(near, 'c', [(0, 1), (1, 0)])]
    pallas_call x1, Pallas kernels: 0.18 us -> 1.2 us  [pack(): pl.pallas_call(pack_body, out_shape=jax.ShapeDtypeStruct((width // HD * p...]
    pallas_call x1 -> x2, Pallas kernels: 5.41 us -> 5.64 us  [the longest x1 3.19 us: attend_far(): pl.pallas_call(functools.partial(far_body, q_rows), out_shape=jax.ShapeDt...]
  transfers between devices with their start and end apart: 1 -> 1, of which waited for: 1 -> 1; matrix products, arithmetic and copies ran while one was open for 0% -> 0% of each run, Pallas kernels for 0% -> 4%
where the time goes in v4:
time: 56.9 us; the launch traced here: 56.7 us
  blocking collectives  48.5 us (85%)
  Pallas kernels  7.59 us (13%)
    all_to_all x1, blocking collectives, local(): near = lax.all_to_all(packed, WIDE, 0, 0, tiled=True)  32 us
    all_to_all x1, blocking collectives, local(): lax.all_to_all(out.reshape(spans * senders, q_rows, HD), WIDE, 0, 0, tile...  16.5 us
    pallas_call x1, Pallas kernels, attend_far(): pl.pallas_call(functools.partial(far_body, q_rows), out_shape=jax.ShapeDt...  3.19 us
    pallas_call x1, Pallas kernels, attend_near(): pl.pallas_call(functools.partial(near_body, q_rows), out_shape=(jax.Shape...  2.44 us
    pallas_call x1, Pallas kernels, pack(): pl.pallas_call(pack_body, out_shape=jax.ShapeDtypeStruct((width // HD * p...  1.2 us
  transfers between devices with their start and end apart: 1, of which 1 were waited for; matrix products, arithmetic and copies ran while one was open for 0% of the time, Pallas kernels for 4%

profile of v4, /device:TPU:0, one launch (start us, length us, event | category | flops | bytes accessed | tf_op | source)
XLA Modules:
  0.0 56.7 jit_solution(4853847876940427742)
XLA Ops:
  0.0 1.2 %pack.1 = bf16[64,80,128]{2,1,0:T(8,128)(2,1)S(1)} custom-call(bf16[32,4096]{1,0:T(8,128)(2,1)} %bitcast.12, bf16[32,4096]{1,0:T(8,128)(2,1)} %bitcast.13, bf16[32,4096]{1,0:T(8,128)(2,1)} %bitcast.14), custom_call_target="tpu_custom_call" | custom-call | tf_op jit(solution)/shard_map/pack/pallas_call | solution.py:51
  1.2 0.0 copy-start.1
  1.2 32.0 %all_to_all.10 = bf16[64,80,128]{2,1,0:T(8,128)(2,1)S(1)} all-to-all(bf16[64,80,128]{2,1,0:T(8,128)(2,1)S(1)} %pack.1), channel_id=1, replica_groups=mesh['yh'=2,'z'=4,'x'=4,'yl'=2,'c'=2] {'yh','z','x','yl'}, dimensions={0} | all-to-all | bytes 2621440 | tf_op jit(solution)/shard_map/all_to_all | solution.py:241
  33.2 0.0 collective-permute-start
  33.2 0.0 copy-done.1
  33.2 0.0 copy-start
  33.2 0.0 copy-start.2
  33.2 2.4 %attend_near.1 = (f32[1024,128]{1,0:T(8,128)S(1)}, f32[1024,1]{1,0:T(8,128)S(1)}, f32[1024,1]{1,0:T(8,128)S(1)}) custom-call(s32[8]{0:T(128)S(1)} %copy-done.1, bf16[8,8,80,128]{3,2,1,0:T(8,128)(2,1)S(1)} %bitcast.8), custom_call_target="tpu_custom_call" | custom-call | flops 1073741824 | bytes 8388608 | tf_op jit(solution)/shard_map/attend_near/pallas_call | solution.py:175
  35.7 0.6 collective-permute-done
  36.2 0.0 copy-done
  36.2 0.0 copy-done.2
  36.2 3.2 %attend_far.1 = bf16[8,8,16,128]{3,2,1,0:T(8,128)(2,1)S(1)} custom-call(s32[8]{0:T(128)S(1)} %copy-done.1, s32[8]{0:T(128)S(1)} %copy-done.2, s32[1]{0:T(128)} %bitcast.head, bf16[8,8,80,128]{3,2,1,0:T(8,128)(2,1)S(1)} %bitcast.9, bf16[8,8,80,128]{3,2,1,0:T(8,128)(2,1)S(1)} %bitcast.10, f32[1024,128]{1,0:T(8,128)S(1)} %get-tuple-element.8.acc_ref, ...), custom_call_target="tpu_custom_call" | custom-call | tf_op jit(solution)/shard_map/attend_far/pallas_call | solution.py:197
  39.4 16.5 %all_to_all.11.a_ref = bf16[64,16,128]{2,1,0:T(8,128)(2,1)S(1)} all-to-all(bf16[64,16,128]{2,1,0:T(8,128)(2,1)S(1)} %bitcast.11), channel_id=1, replica_groups=mesh['yh'=2,'z'=4,'x'=4,'yl'=2,'c'=2] {'yh','z','x','yl'}, dimensions={0} | all-to-all | bytes 524288 | tf_op jit(solution)/shard_map/all_to_all | solution.py:248
  56.0 0.7 %unpack.1 = bf16[32,4096]{1,0:T(8,128)(2,1)} custom-call(bf16[64,16,128]{2,1,0:T(8,128)(2,1)S(1)} %all_to_all.11.a_ref), custom_call_target="tpu_custom_call" | custom-call | tf_op jit(solution)/shard_map/unpack/pallas_call | solution.py:224
Async XLA Ops:
  1.2 32.0 %copy-start.1 = (s32[8]{0:T(128)S(1)}, s32[8]{0:T(128)}, u32[]{:S(2)}) copy-start(s32[8]{0:T(128)} %rank.3) | copy-start | bytes 100
  33.2 3.0 %collective-permute-start = (bf16[64,80,128]{2,1,0:T(8,128)(2,1)S(1)}, bf16[64,80,128]{2,1,0:T(8,128)(2,1)S(1)}, u32[]{:S(2)}, u32[]{:S(2)}) collective-permute-start(bf16[64,80,128]{2,1,0:T(8,128)(2,1)S(1)} %all_to_all.10), channel_id=1, source_target_pairs={{0,1},{1,0},{2,3},{3,2},{4,5},{5,4},{6,7},{7,6},{8,9},{9,8},{10,11... | collective-permute-start | bytes 3932168 | tf_op jit(solution)/shard_map/ppermute | solution.py:242
  33.2 3.0 %copy-start = (f32[50,4096]{1,0:T(8,128)S(1)}, f32[50,4096]{1,0:T(8,128)}, u32[]{:S(2)}) copy-start(f32[50,4096]{1,0:T(8,128)} %gate_ref.1) | copy-start | bytes 2457604
  33.2 3.0 %copy-start.2 = (s32[8]{0:T(128)S(1)}, s32[8]{0:T(128)}, u32[]{:S(2)}) copy-start(s32[8]{0:T(128)} %levels.1) | copy-start | bytes 100

commit v5 on v4

--- a/solution.py
+++ b/solution.py
@@ -9,10 +9,12 @@
 from jax.sharding import PartitionSpec as P
 
 HD = 128
-AXES = ("yh", "z", "x", "yl", "c")
-SIZES = (2, 4, 4, 2, 2)
-HEAD_AXES = ("yh", "z", "x")
-WIDE = ("yh", "z", "x", "yl")
+AXES = ("y1", "z1", "z0", "x1", "x0", "y0", "c")
+SPAN_AXES = AXES[:3]
+SEQ_AXES = AXES[3:]
+WIDE = ("x1", "x0", "y1", "y0", "z1", "z0")
+HEAD_AXES = WIDE[:-1]
+PARTS = 2
 MIB = 1 << 20
 VMEM_WHOLE = pl.BlockSpec(memory_space=pltpu.VMEM)
 SMEM_WHOLE = pl.BlockSpec(memory_space=pltpu.SMEM)
@@ -62,6 +64,14 @@
     )(*(pltpu.with_memory_space_constraint(a, pltpu.HBM) for a in (q, k, v)))
 
 
+def sent_by(span):
+    bits = len(SPAN_AXES)
+    return tuple(
+        (span >> (bits - 1 - SPAN_AXES.index(axis))) & 1 if axis in SPAN_AXES else slice(None)
+        for axis in WIDE
+    )
+
+
 def span_order(rank, spans):
     order = []
     for place in range(spans):
@@ -72,21 +82,33 @@
     return order
 
 
-def score_visible(order, q_ref, kv_ref, q_rows, q_s, s_s):
-    spans, senders, packed, hd = kv_ref.shape
+def take(ref, span, start, stop):
+    hd = ref.shape[-1]
+    block = ref[sent_by(span) + (slice(start, stop), slice(None))]
+    return block.reshape(block.size // hd, hd)
+
+
+def sizes(rank, ref):
+    spans = rank.shape[0]
+    senders = 2 ** len(WIDE) // spans
+    return spans, senders, ref.shape[-2], ref.shape[-1]
+
+
+def score_visible(order, shape, q_ref, kv_ref, q_rows, q_s, s_s):
+    spans, senders, packed, hd = shape
     rows = (packed - q_rows) // 2
     q_step, k_step = senders * q_rows, senders * rows
     for r in range(spans):
-        q_s[r * q_step : (r + 1) * q_step, :] = q_ref[order[r], :, 0:q_rows, :].reshape(q_step, hd)
+        q_s[r * q_step : (r + 1) * q_step, :] = take(q_ref, order[r], 0, q_rows)
     for b in range(spans):
-        k = kv_ref[order[b], :, q_rows : q_rows + rows, :].reshape(k_step, hd)
+        k = take(kv_ref, order[b], q_rows, q_rows + rows)
         s_s[b * q_step :, b * k_step : (b + 1) * k_step] = lax.dot_general(
             q_s[b * q_step :, :], k, ROW_BY_ROW, preferred_element_type=jnp.float32
         )
 
 
-def weighted_values(order, g, group, kv_ref, q_rows, p_s):
-    spans, senders, packed, hd = kv_ref.shape
+def weighted_values(order, shape, g, group, kv_ref, q_rows, p_s):
+    spans, senders, packed, hd = shape
     rows = (packed - q_rows) // 2
     q_step, k_step = senders * q_rows, senders * rows
     for a in range(group - 1):
@@ -96,7 +118,7 @@
         )
     acc = None
     for b in range((g + 1) * group):
-        v = kv_ref[order[b], :, q_rows + rows :, :].reshape(k_step, hd)
+        v = take(kv_ref, order[b], q_rows + rows, packed)
         part = jnp.dot(
             p_s[g * group * q_step : (g + 1) * group * q_step, b * k_step : (b + 1) * k_step],
             v,
@@ -107,11 +129,11 @@
 
 
 def near_body(q_rows, rank, near_ref, acc_ref, top_ref, total_ref, q_s, s_s, p_s):
-    spans, senders, packed, hd = near_ref.shape
+    shape = spans, senders, packed, hd = sizes(rank, near_ref)
     q_step, k_step = senders * q_rows, senders * (packed - q_rows) // 2
     factor = LOG2E / hd**0.5
     order = span_order(rank, spans)
-    score_visible(order, near_ref, near_ref, q_rows, q_s, s_s)
+    score_visible(order, shape, near_ref, near_ref, q_rows, q_s, s_s)
     for r in range(spans):
         here = slice(r * q_step, (r + 1) * q_step)
         s = s_s[here, 0 : (r + 1) * k_step]
@@ -122,7 +144,7 @@
         p_s[here, 0 : (r + 1) * k_step] = e.astype(p_s.dtype)
     for g in range(spans // 2):
         acc_ref[2 * g * q_step : 2 * (g + 1) * q_step, :] = weighted_values(
-            order, g, 2, near_ref, q_rows, p_s
+            order, shape, g, 2, near_ref, q_rows, p_s
         )
 
 
@@ -130,14 +152,14 @@
     q_rows, rank, levels, head, near_ref, far_ref, acc_ref, top_ref, total_ref, gate_ref,
     o_ref, q_s, s_s, p_s, g_s, scale_s, total_s, sem,
 ):
-    spans, senders, packed, hd = near_ref.shape
+    shape = spans, senders, packed, hd = sizes(rank, near_ref)
     q_step, k_step = senders * q_rows, senders * (packed - q_rows) // 2
     factor = LOG2E / hd**0.5
     columns = pl.ds(pl.multiple_of(head[0] * hd, hd), hd)
     fetch = pltpu.make_async_copy(gate_ref.at[:, columns], g_s, sem)
     fetch.start()
     order = span_order(rank, spans)
-    score_visible(order, near_ref, far_ref, q_rows, q_s, s_s)
+    score_visible(order, shape, near_ref, far_ref, q_rows, q_s, s_s)
     for r in range(spans):
         here = slice(r * q_step, (r + 1) * q_step)
         s = s_s[here, 0 : (r + 1) * k_step]
@@ -149,14 +171,16 @@
         p_s[here, 0 : (r + 1) * k_step] = e.astype(p_s.dtype)
     fetch.wait()
     for g in range(spans // 2):
-        acc = weighted_values(order, g, 2, far_ref, q_rows, p_s)
+        acc = weighted_values(order, shape, g, 2, far_ref, q_rows, p_s)
         for a in range(2):
             r = 2 * g + a
             here = slice(r * q_step, (r + 1) * q_step)
             both = acc_ref[here, :] * scale_s[here, :] + acc[a * q_step : (a + 1) * q_step, :]
             attended = (both / total_s[here, :]).astype(jnp.bfloat16).astype(jnp.float32)
             gated = (g_s[pl.ds(levels[order[r]], 1), :] * attended).astype(o_ref.dtype)
-            o_ref[order[r]] = gated.reshape(senders, q_rows, hd)
+            home = sent_by(order[r])
+            free = tuple(2 for at in home if isinstance(at, slice))
+            o_ref[home + (slice(None), slice(None))] = gated.reshape(free + (q_rows, hd))
 
 
 def attend_scratch(spans, senders, q_rows, rows, hd, dtype):
@@ -169,7 +193,7 @@
 
 
 def attend_near(rank, near, q_rows):
-    spans, senders, packed, hd = near.shape
+    spans, senders, packed, hd = sizes(rank, near)
     rows = (packed - q_rows) // 2
     q_total, k_total = spans * senders * q_rows, spans * senders * rows
     return pl.pallas_call(
@@ -191,12 +215,12 @@
 
 
 def attend_far(rank, levels, head, near, far, acc, top, total, gate_table, q_rows):
-    spans, senders, packed, hd = near.shape
+    spans, senders, packed, hd = sizes(rank, near)
     rows = (packed - q_rows) // 2
     q_total = spans * senders * q_rows
     return pl.pallas_call(
         functools.partial(far_body, q_rows),
-        out_shape=jax.ShapeDtypeStruct((spans, senders, q_rows, hd), near.dtype),
+        out_shape=jax.ShapeDtypeStruct(near.shape[:-2] + (q_rows, hd), near.dtype),
         in_specs=[SMEM_WHOLE] * 3 + [VMEM_WHOLE] * 5 + [HBM_WHOLE],
         out_specs=VMEM_WHOLE,
         scratch_shapes=attend_scratch(spans, senders, q_rows, rows, hd, near.dtype)
@@ -232,26 +256,23 @@
 
 
 def local(queries, keys, values, gate_table, levels, span_rank):
-    spans = span_rank.shape[0]
     rows = queries.shape[1]
-    parts = SIZES[3]
-    q_rows = rows // parts
+    q_rows = rows // PARTS
     head = lax.axis_index(HEAD_AXES).astype(jnp.int32).reshape(1)
-    packed = pack(queries[0], keys[0], values[0], parts)
+    packed = pack(queries[0], keys[0], values[0], PARTS)
     near = lax.all_to_all(packed, WIDE, 0, 0, tiled=True)
     far = lax.ppermute(near, "c", [(0, 1), (1, 0)])
-    senders = near.shape[0] // spans
-    shape = (spans, senders) + near.shape[1:]
+    shape = (2,) * len(WIDE) + near.shape[1:]
     near, far = near.reshape(shape), far.reshape(shape)
     part = attend_near(span_rank, near, q_rows)
     out = attend_far(span_rank, levels, head, near, far, *part, gate_table, q_rows)
-    back = lax.all_to_all(out.reshape(spans * senders, q_rows, HD), WIDE, 0, 0, tiled=True)
+    back = lax.all_to_all(out.reshape((-1,) + out.shape[-2:]), WIDE, 0, 0, tiled=True)
     return unpack(back, rows)[None]
 
 
 def solution(mesh):
-    fine = Mesh(mesh.devices.reshape(SIZES), AXES)
-    split = P(("yh", "z"), ("x", "yl", "c"), None)
+    fine = Mesh(mesh.devices.reshape((2,) * len(AXES)), AXES)
+    split = P(SPAN_AXES, SEQ_AXES, None)
     return jax.shard_map(
         local,
         mesh=fine,

time: 56.9 us -> 56.2 us (0.988)
  blocking collectives: 48.5 us -> 47.8 us
    all_to_all x1, blocking collectives: 16.5 us -> 15 us  [local(): lax.all_to_all(out.reshape((-1,) + out.shape[-2:]), WIDE, 0, 0, tiled=True)]
    all_to_all x1, blocking collectives: 32 us -> 32.8 us  [local(): near = lax.all_to_all(packed, WIDE, 0, 0, tiled=True)]
where the time goes in v5:
time: 56.2 us; the launch traced here: 56 us
  blocking collectives  47.8 us (85%)
  Pallas kernels  7.63 us (14%)
    all_to_all x1, blocking collectives, local(): near = lax.all_to_all(packed, WIDE, 0, 0, tiled=True)  32.8 us
    all_to_all x1, blocking collectives, local(): lax.all_to_all(out.reshape((-1,) + out.shape[-2:]), WIDE, 0, 0, tiled=True)  15 us
    pallas_call x1, Pallas kernels, attend_far(): pl.pallas_call(functools.partial(far_body, q_rows), out_shape=jax.ShapeDt...  3.19 us
    pallas_call x1, Pallas kernels, attend_near(): pl.pallas_call(functools.partial(near_body, q_rows), out_shape=(jax.Shape...  2.49 us
    pallas_call x1, Pallas kernels, pack(): pl.pallas_call(pack_body, out_shape=jax.ShapeDtypeStruct((width // HD * p...  1.2 us
  transfers between devices with their start and end apart: 1, of which 1 were waited for; matrix products, arithmetic and copies ran while one was open for 0% of the time, Pallas kernels for 4%

profile of v5, /device:TPU:0, one launch (start us, length us, event | category | flops | bytes accessed | tf_op | source)
XLA Modules:
  0.0 56.0 jit_solution(8616397711829514278)
XLA Ops:
  0.0 1.2 %pack.1 = bf16[64,80,128]{2,1,0:T(8,128)(2,1)S(1)} custom-call(bf16[32,4096]{1,0:T(8,128)(2,1)} %bitcast.12, bf16[32,4096]{1,0:T(8,128)(2,1)} %bitcast.13, bf16[32,4096]{1,0:T(8,128)(2,1)} %bitcast.14), custom_call_target="tpu_custom_call" | custom-call | tf_op jit(solution)/shard_map/pack/pallas_call | solution.py:53
  1.2 0.0 copy-start.1
  1.2 32.8 %all_to_all.10 = bf16[64,80,128]{2,1,0:T(8,128)(2,1)S(1)} all-to-all(bf16[64,80,128]{2,1,0:T(8,128)(2,1)S(1)} %pack.1), channel_id=1, replica_groups=mesh['y1'=2,'z1'=2,'z0'=2,'x1'=2,'x0'=2,'y0'=2,'c'=2] {'x1','x0','y1','y..., dimensions={0} | all-to-all | bytes 2621440 | tf_op jit(solution)/shard_map/all_to_all | solution.py:263
  34.0 0.0 collective-permute-start
  34.0 0.0 copy-done.1
  34.0 0.0 copy-start
  34.0 0.0 copy-start.2
  34.0 2.5 %attend_near.1 = (f32[1024,128]{1,0:T(8,128)S(1)}, f32[1024,1]{1,0:T(8,128)S(1)}, f32[1024,1]{1,0:T(8,128)S(1)}) custom-call(s32[8]{0:T(128)S(1)} %copy-done.1, bf16[2,2,2,2,2,2,80,128]{7,6,5,4,3,2,1,0:T(8,128)(2,1)S(1)} %bitcast.8), custom_call_target="tpu_custom_call" | custom-call | flops 1073741824 | bytes 8388608 | tf_op jit(solution)/shard_map/attend_near/pallas_call | solution.py:199
  36.5 0.5 collective-permute-done
  37.0 0.0 copy-done
  37.0 0.0 copy-done.2
  37.0 3.2 %attend_far.1 = bf16[2,2,2,2,2,2,16,128]{7,6,5,4,3,2,1,0:T(8,128)(2,1)S(1)} custom-call(s32[8]{0:T(128)S(1)} %copy-done.1, s32[8]{0:T(128)S(1)} %copy-done.2, s32[1]{0:T(128)} %bitcast.head, bf16[2,2,2,2,2,2,80,128]{7,6,5,4,3,2,1,0:T(8,128)(2,1)S(1)} %bitcast.9, bf16[2,2,2,2,2,2,80,128]{7,6,5,4,3,2,1,0:T(8,128)(2,1)S(1)} %bitcast.10, ...), custom_call_target="tpu_custom_call" | custom-call | tf_op jit(solution)/shard_map/attend_far/pallas_call | solution.py:221
  40.2 15.0 %all_to_all.11.a_ref = bf16[64,16,128]{2,1,0:T(8,128)(2,1)S(1)} all-to-all(bf16[64,16,128]{2,1,0:T(8,128)(2,1)S(1)} %bitcast.11), channel_id=1, replica_groups=mesh['y1'=2,'z1'=2,'z0'=2,'x1'=2,'x0'=2,'y0'=2,'c'=2] {'x1','x0','y1','y..., dimensions={0} | all-to-all | bytes 524288 | tf_op jit(solution)/shard_map/all_to_all | solution.py:269
  55.3 0.7 %unpack.1 = bf16[32,4096]{1,0:T(8,128)(2,1)} custom-call(bf16[64,16,128]{2,1,0:T(8,128)(2,1)S(1)} %all_to_all.11.a_ref), custom_call_target="tpu_custom_call" | custom-call | tf_op jit(solution)/shard_map/unpack/pallas_call | solution.py:248
Async XLA Ops:
  1.2 32.8 %copy-start.1 = (s32[8]{0:T(128)S(1)}, s32[8]{0:T(128)}, u32[]{:S(2)}) copy-start(s32[8]{0:T(128)} %rank.3) | copy-start | bytes 100
  34.0 3.0 %collective-permute-start = (bf16[64,80,128]{2,1,0:T(8,128)(2,1)S(1)}, bf16[64,80,128]{2,1,0:T(8,128)(2,1)S(1)}, u32[]{:S(2)}, u32[]{:S(2)}) collective-permute-start(bf16[64,80,128]{2,1,0:T(8,128)(2,1)S(1)} %all_to_all.10), channel_id=1, source_target_pairs={{0,1},{1,0},{2,3},{3,2},{4,5},{5,4},{6,7},{7,6},{8,9},{9,8},{10,11... | collective-permute-start | bytes 3932168 | tf_op jit(solution)/shard_map/ppermute | solution.py:264
  34.0 3.0 %copy-start = (f32[50,4096]{1,0:T(8,128)S(1)}, f32[50,4096]{1,0:T(8,128)}, u32[]{:S(2)}) copy-start(f32[50,4096]{1,0:T(8,128)} %gate_ref.1) | copy-start | bytes 2457604
  34.0 3.0 %copy-start.2 = (s32[8]{0:T(128)S(1)}, s32[8]{0:T(128)}, u32[]{:S(2)}) copy-start(s32[8]{0:T(128)} %levels.1) | copy-start | bytes 100

commit v6 on v5

--- a/solution.py
+++ b/solution.py
@@ -94,102 +94,124 @@
     return spans, senders, ref.shape[-2], ref.shape[-1]
 
 
-def score_visible(order, shape, q_ref, kv_ref, q_rows, q_s, s_s):
+def attend_blocks(order, shape, q_ref, kv_ref, q_rows, s_s, past_top, finish):
     spans, senders, packed, hd = shape
     rows = (packed - q_rows) // 2
     q_step, k_step = senders * q_rows, senders * rows
-    for r in range(spans):
-        q_s[r * q_step : (r + 1) * q_step, :] = take(q_ref, order[r], 0, q_rows)
-    for b in range(spans):
-        k = take(kv_ref, order[b], q_rows, q_rows + rows)
-        s_s[b * q_step :, b * k_step : (b + 1) * k_step] = lax.dot_general(
-            q_s[b * q_step :, :], k, ROW_BY_ROW, preferred_element_type=jnp.float32
-        )
-
-
-def weighted_values(order, shape, g, group, kv_ref, q_rows, p_s):
-    spans, senders, packed, hd = shape
-    rows = (packed - q_rows) // 2
-    q_step, k_step = senders * q_rows, senders * rows
-    for a in range(group - 1):
-        r = g * group + a
-        p_s[r * q_step : (r + 1) * q_step, (r + 1) * k_step : (g + 1) * group * k_step] = jnp.zeros(
-            (q_step, (group - 1 - a) * k_step), p_s.dtype
-        )
-    acc = None
-    for b in range((g + 1) * group):
-        v = take(kv_ref, order[b], q_rows + rows, packed)
-        part = jnp.dot(
-            p_s[g * group * q_step : (g + 1) * group * q_step, b * k_step : (b + 1) * k_step],
-            v,
+    factor = LOG2E / hd**0.5
+    lanes = [slice(i * hd, (i + 1) * hd) for i in range(k_step // hd)]
+
+    def members(g, b):
+        return (0, 1) if b <= 2 * g else (1,)
+
+    def span_rows(which):
+        return slice(which[0] * q_step, (which[-1] + 1) * q_step)
+
+    def score(g, b, queries, tops):
+        which = members(g, b)
+        scores = lax.dot_general(
+            queries[span_rows(which), :],
+            take(kv_ref, order[b], q_rows, q_rows + rows),
+            ROW_BY_ROW,
             preferred_element_type=jnp.float32,
         )
-        acc = part if acc is None else acc + part
-    return acc
-
-
-def near_body(q_rows, rank, near_ref, acc_ref, top_ref, total_ref, q_s, s_s, p_s):
+        s_s[g % 2][span_rows(which), b * k_step : (b + 1) * k_step] = scores
+        for n, a in enumerate(which):
+            for at in lanes:
+                part = scores[n * q_step : (n + 1) * q_step, at]
+                tops[a] = part if tops[a] is None else jnp.maximum(tops[a], part)
+
+    def weigh(g, b, top, sums):
+        which = members(g, b)
+        values = take(kv_ref, order[b], q_rows + rows, packed)
+        values = jnp.concatenate([values, jnp.ones_like(values)], axis=1)
+        weights = []
+        for a in which:
+            s = s_s[g % 2][span_rows((a,)), b * k_step : (b + 1) * k_step]
+            parts = [
+                jnp.exp2((s[:, at] - top[a]) * factor).astype(jnp.bfloat16) for at in lanes
+            ]
+            weights.append(jnp.concatenate(parts, axis=1))
+        w = weights[0] if len(weights) == 1 else jnp.concatenate(weights, axis=0)
+        part = jnp.dot(w, values, preferred_element_type=jnp.float32)
+        for n, a in enumerate(which):
+            piece = part[n * q_step : (n + 1) * q_step, :]
+            sums[a] = piece if sums[a] is None else sums[a] + piece
+
+    def queries_of(g):
+        return jnp.concatenate(
+            [take(q_ref, order[2 * g + a], 0, q_rows) for a in range(2)], axis=0
+        )
+
+    last = spans // 2 - 1
+    queries, tops = queries_of(last), [None, None]
+    for b in range(2 * last + 2):
+        score(last, b, queries, tops)
+    for g in range(last, -1, -1):
+        top = []
+        for a in range(2):
+            most = jnp.broadcast_to(jnp.max(tops[a], axis=1, keepdims=True), tops[a].shape)
+            top.append(most if past_top is None else jnp.maximum(most, past_top(2 * g + a)))
+        sums, tops = [None, None], [None, None]
+        if g > 0:
+            queries = queries_of(g - 1)
+        for b in range(2 * g + 2):
+            if b < 2 * g:
+                score(g - 1, b, queries, tops)
+            weigh(g, b, top, sums)
+        for a in range(2):
+            finish(2 * g + a, top[a], sums[a][:, hd:], sums[a][:, 0:hd])
+
+
+def near_body(q_rows, rank, near_ref, acc_ref, top_ref, total_ref, even_s, odd_s):
     shape = spans, senders, packed, hd = sizes(rank, near_ref)
-    q_step, k_step = senders * q_rows, senders * (packed - q_rows) // 2
-    factor = LOG2E / hd**0.5
+    q_step = senders * q_rows
     order = span_order(rank, spans)
-    score_visible(order, shape, near_ref, near_ref, q_rows, q_s, s_s)
-    for r in range(spans):
+
+    def finish(r, top, total, acc):
         here = slice(r * q_step, (r + 1) * q_step)
-        s = s_s[here, 0 : (r + 1) * k_step]
-        top = jnp.max(s, axis=1, keepdims=True)
-        e = jnp.exp2((s - top) * factor)
+        acc_ref[here, :] = acc
         top_ref[here, :] = top
-        total_ref[here, :] = jnp.sum(e, axis=1, keepdims=True)
-        p_s[here, 0 : (r + 1) * k_step] = e.astype(p_s.dtype)
-    for g in range(spans // 2):
-        acc_ref[2 * g * q_step : 2 * (g + 1) * q_step, :] = weighted_values(
-            order, shape, g, 2, near_ref, q_rows, p_s
-        )
+        total_ref[here, :] = total
+
+    attend_blocks(order, shape, near_ref, near_ref, q_rows, (even_s, odd_s), None, finish)
 
 
 def far_body(
     q_rows, rank, levels, head, near_ref, far_ref, acc_ref, top_ref, total_ref, gate_ref,
-    o_ref, q_s, s_s, p_s, g_s, scale_s, total_s, sem,
+    o_ref, even_s, odd_s, g_s, sem,
 ):
     shape = spans, senders, packed, hd = sizes(rank, near_ref)
-    q_step, k_step = senders * q_rows, senders * (packed - q_rows) // 2
+    q_step = senders * q_rows
     factor = LOG2E / hd**0.5
     columns = pl.ds(pl.multiple_of(head[0] * hd, hd), hd)
     fetch = pltpu.make_async_copy(gate_ref.at[:, columns], g_s, sem)
     fetch.start()
     order = span_order(rank, spans)
-    score_visible(order, shape, near_ref, far_ref, q_rows, q_s, s_s)
-    for r in range(spans):
+    arrived = []
+
+    def past_top(r):
+        return top_ref[r * q_step : (r + 1) * q_step, :]
+
+    def finish(r, top, total, acc):
+        if not arrived:
+            fetch.wait()
+            arrived.append(r)
         here = slice(r * q_step, (r + 1) * q_step)
-        s = s_s[here, 0 : (r + 1) * k_step]
-        top = jnp.maximum(jnp.max(s, axis=1, keepdims=True), top_ref[here, :])
-        e = jnp.exp2((s - top) * factor)
         scale = jnp.exp2((top_ref[here, :] - top) * factor)
-        scale_s[here, :] = scale
-        total_s[here, :] = total_ref[here, :] * scale + jnp.sum(e, axis=1, keepdims=True)
-        p_s[here, 0 : (r + 1) * k_step] = e.astype(p_s.dtype)
-    fetch.wait()
-    for g in range(spans // 2):
-        acc = weighted_values(order, shape, g, 2, far_ref, q_rows, p_s)
-        for a in range(2):
-            r = 2 * g + a
-            here = slice(r * q_step, (r + 1) * q_step)
-            both = acc_ref[here, :] * scale_s[here, :] + acc[a * q_step : (a + 1) * q_step, :]
-            attended = (both / total_s[here, :]).astype(jnp.bfloat16).astype(jnp.float32)
-            gated = (g_s[pl.ds(levels[order[r]], 1), :] * attended).astype(o_ref.dtype)
-            home = sent_by(order[r])
-            free = tuple(2 for at in home if isinstance(at, slice))
-            o_ref[home + (slice(None), slice(None))] = gated.reshape(free + (q_rows, hd))
-
-
-def attend_scratch(spans, senders, q_rows, rows, hd, dtype):
-    q_total, k_total = spans * senders * q_rows, spans * senders * rows
-    return [
-        pltpu.VMEM((q_total, hd), dtype),
-        pltpu.VMEM((q_total, k_total), jnp.float32),
-        pltpu.VMEM((q_total, k_total), dtype),
-    ]
+        both = acc_ref[here, :] * scale + acc
+        attended = both / (total_ref[here, :] * scale + total)
+        attended = attended.astype(jnp.bfloat16).astype(jnp.float32)
+        gated = (g_s[pl.ds(levels[order[r]], 1), :] * attended).astype(o_ref.dtype)
+        home = sent_by(order[r])
+        free = tuple(2 for at in home if isinstance(at, slice))
+        o_ref[home + (slice(None), slice(None))] = gated.reshape(free + (q_rows, hd))
+
+    attend_blocks(order, shape, near_ref, far_ref, q_rows, (even_s, odd_s), past_top, finish)
+
+
+def score_scratch(spans, senders, q_rows, rows):
+    return [pltpu.VMEM((2 * senders * q_rows, spans * senders * rows), jnp.float32)] * 2
 
 
 def attend_near(rank, near, q_rows):
@@ -200,12 +222,12 @@
         functools.partial(near_body, q_rows),
         out_shape=(
             jax.ShapeDtypeStruct((q_total, hd), jnp.float32),
-            jax.ShapeDtypeStruct((q_total, 1), jnp.float32),
-            jax.ShapeDtypeStruct((q_total, 1), jnp.float32),
+            jax.ShapeDtypeStruct((q_total, hd), jnp.float32),
+            jax.ShapeDtypeStruct((q_total, hd), jnp.float32),
         ),
         in_specs=[SMEM_WHOLE, VMEM_WHOLE],
         out_specs=(VMEM_WHOLE,) * 3,
-        scratch_shapes=attend_scratch(spans, senders, q_rows, rows, hd, near.dtype),
+        scratch_shapes=score_scratch(spans, senders, q_rows, rows),
         compiler_params=pltpu.CompilerParams(vmem_limit_bytes=24 * MIB),
         cost_estimate=pl.CostEstimate(
             flops=4 * q_total * k_total * hd, bytes_accessed=8 * MIB, transcendentals=0
@@ -223,11 +245,9 @@
         out_shape=jax.ShapeDtypeStruct(near.shape[:-2] + (q_rows, hd), near.dtype),
         in_specs=[SMEM_WHOLE] * 3 + [VMEM_WHOLE] * 5 + [HBM_WHOLE],
         out_specs=VMEM_WHOLE,
-        scratch_shapes=attend_scratch(spans, senders, q_rows, rows, hd, near.dtype)
+        scratch_shapes=score_scratch(spans, senders, q_rows, rows)
         + [
             pltpu.VMEM((gate_table.shape[0], hd), gate_table.dtype),
-            pltpu.VMEM((q_total, 1), jnp.float32),
-            pltpu.VMEM((q_total, 1), jnp.float32),
             pltpu.SemaphoreType.DMA,
         ],
         compiler_params=pltpu.CompilerParams(vmem_limit_bytes=24 * MIB),

time: 56.2 us -> 55.8 us (level)
  no operation moved by 1% of the time
where the time goes in v6:
time: 55.8 us; the launch traced here: 55.6 us
  blocking collectives  47.8 us (86%)
  Pallas kernels  7.12 us (13%)
  waiting for transfers between devices  0.6 us (1%)
    all_to_all x1, blocking collectives, local(): near = lax.all_to_all(packed, WIDE, 0, 0, tiled=True)  32.8 us
    all_to_all x1, blocking collectives, local(): lax.all_to_all(out.reshape((-1,) + out.shape[-2:]), WIDE, 0, 0, tiled=True)  15 us
    pallas_call x1, Pallas kernels, attend_far(): pl.pallas_call(functools.partial(far_body, q_rows), out_shape=jax.ShapeDt...  2.77 us
    pallas_call x1, Pallas kernels, attend_near(): pl.pallas_call(functools.partial(near_body, q_rows), out_shape=(jax.Shape...  2.4 us
    pallas_call x1, Pallas kernels, pack(): pl.pallas_call(pack_body, out_shape=jax.ShapeDtypeStruct((width // HD * p...  1.2 us
  transfers between devices with their start and end apart: 1, of which 1 were waited for; matrix products, arithmetic and copies ran while one was open for 0% of the time, Pallas kernels for 4%

profile of v6, /device:TPU:0, one launch (start us, length us, event | category | flops | bytes accessed | tf_op | source)
XLA Modules:
  0.0 55.6 jit_solution(3413522360388804350)
XLA Ops:
  0.0 1.2 %pack.1 = bf16[64,80,128]{2,1,0:T(8,128)(2,1)S(1)} custom-call(bf16[32,4096]{1,0:T(8,128)(2,1)} %bitcast.12, bf16[32,4096]{1,0:T(8,128)(2,1)} %bitcast.13, bf16[32,4096]{1,0:T(8,128)(2,1)} %bitcast.14), custom_call_target="tpu_custom_call" | custom-call | tf_op jit(solution)/shard_map/pack/pallas_call | solution.py:53
  1.2 0.0 copy-start.1
  1.2 32.8 %all_to_all.10 = bf16[64,80,128]{2,1,0:T(8,128)(2,1)S(1)} all-to-all(bf16[64,80,128]{2,1,0:T(8,128)(2,1)S(1)} %pack.1), channel_id=1, replica_groups=mesh['y1'=2,'z1'=2,'z0'=2,'x1'=2,'x0'=2,'y0'=2,'c'=2] {'x1','x0','y1','y..., dimensions={0} | all-to-all | bytes 2621440 | tf_op jit(solution)/shard_map/all_to_all | solution.py:283
  34.0 0.0 collective-permute-start
  34.0 0.0 copy-done.1
  34.0 0.0 copy-start
  34.0 0.0 copy-start.2
  34.0 2.4 %attend_near.1 = (f32[1024,128]{1,0:T(8,128)S(1)}, f32[1024,128]{1,0:T(8,128)S(1)}, f32[1024,128]{1,0:T(8,128)S(1)}) custom-call(s32[8]{0:T(128)S(1)} %copy-done.1, bf16[2,2,2,2,2,2,80,128]{7,6,5,4,3,2,1,0:T(8,128)(2,1)S(1)} %bitcast.8), custom_call_target="tpu_custom_call" | custom-call | flops 1073741824 | bytes 8388608 | tf_op jit(solution)/shard_map/attend_near/pallas_call | solution.py:221
  36.4 0.6 %collective-permute-done = bf16[64,80,128]{2,1,0:T(8,128)(2,1)S(1)} collective-permute-done((bf16[64,80,128]{2,1,0:T(8,128)(2,1)S(1)}, bf16[64,80,128]{2,1,0:T(8,128)(2,1)S(1)}, u32[]{:S(2)}, u32[]{:S(2)}) %collective-permute-start) | collective-permute-done | bytes 1310752 | tf_op jit(solution)/shard_map/ppermute | solution.py:284
  37.0 0.0 copy-done
  37.0 0.0 copy-done.2
  37.0 2.8 %attend_far.1 = bf16[2,2,2,2,2,2,16,128]{7,6,5,4,3,2,1,0:T(8,128)(2,1)S(1)} custom-call(s32[8]{0:T(128)S(1)} %copy-done.1, s32[8]{0:T(128)S(1)} %copy-done.2, s32[1]{0:T(128)} %bitcast.head, bf16[2,2,2,2,2,2,80,128]{7,6,5,4,3,2,1,0:T(8,128)(2,1)S(1)} %bitcast.9, bf16[2,2,2,2,2,2,80,128]{7,6,5,4,3,2,1,0:T(8,128)(2,1)S(1)} %bitcast.10, ...), custom_call_target="tpu_custom_call" | custom-call | tf_op jit(solution)/shard_map/attend_far/pallas_call | solution.py:243
  39.8 15.0 %all_to_all.11.a_ref = bf16[64,16,128]{2,1,0:T(8,128)(2,1)S(1)} all-to-all(bf16[64,16,128]{2,1,0:T(8,128)(2,1)S(1)} %bitcast.11), channel_id=1, replica_groups=mesh['y1'=2,'z1'=2,'z0'=2,'x1'=2,'x0'=2,'y0'=2,'c'=2] {'x1','x0','y1','y..., dimensions={0} | all-to-all | bytes 524288 | tf_op jit(solution)/shard_map/all_to_all | solution.py:289
  54.8 0.7 %unpack.1 = bf16[32,4096]{1,0:T(8,128)(2,1)} custom-call(bf16[64,16,128]{2,1,0:T(8,128)(2,1)S(1)} %all_to_all.11.a_ref), custom_call_target="tpu_custom_call" | custom-call | tf_op jit(solution)/shard_map/unpack/pallas_call | solution.py:268
Async XLA Ops:
  1.2 32.8 %copy-start.1 = (s32[8]{0:T(128)S(1)}, s32[8]{0:T(128)}, u32[]{:S(2)}) copy-start(s32[8]{0:T(128)} %rank.3) | copy-start | bytes 100
  34.0 3.0 %collective-permute-start = (bf16[64,80,128]{2,1,0:T(8,128)(2,1)S(1)}, bf16[64,80,128]{2,1,0:T(8,128)(2,1)S(1)}, u32[]{:S(2)}, u32[]{:S(2)}) collective-permute-start(bf16[64,80,128]{2,1,0:T(8,128)(2,1)S(1)} %all_to_all.10), channel_id=1, source_target_pairs={{0,1},{1,0},{2,3},{3,2},{4,5},{5,4},{6,7},{7,6},{8,9},{9,8},{10,11... | collective-permute-start | bytes 3932168 | tf_op jit(solution)/shard_map/ppermute | solution.py:284
  34.0 3.0 %copy-start = (f32[50,4096]{1,0:T(8,128)S(1)}, f32[50,4096]{1,0:T(8,128)}, u32[]{:S(2)}) copy-start(f32[50,4096]{1,0:T(8,128)} %gate_ref.1) | copy-start | bytes 2457604
  34.0 3.0 %copy-start.2 = (s32[8]{0:T(128)S(1)}, s32[8]{0:T(128)}, u32[]{:S(2)}) copy-start(s32[8]{0:T(128)} %levels.1) | copy-start | bytes 100
